TPU v7x, 32 devices: a whole 2x2x4 slice. The times are simulated.
32 devices in a mesh: dp: 8 (over z, x), tensor: 4 (over y, core).
Axes of the slice: x: 2, y: 2, z: 4, core: 2. Of those that a mesh axis runs over, the one named last changes fastest.
Arguments:
- tokens: bfloat16 [7584, 768], P('dp'), may hold values from -6 to 6
- token_mask: int32 [7584], P('dp'), may hold values from 0 to 1, as said below
- expert_type: int32 [7584], P('dp'), may hold values from 0 to 1, as said below
- cotangent: bfloat16 [7584, 768], P('dp'), may hold values from -6 to 6
- ln1_gain: float32 [768], replicated, may hold values from 0.5 to 1.5
- ln1_bias: float32 [768], replicated, may hold values from -0.6 to 0.6
- w_qkv: bfloat16 [768, 3, 768], P(None, None, 'tensor'), may hold values from -0.21875 to 0.21875
- qv_bias: float32 [2, 768], P(None, 'tensor'), may hold values from -0.6 to 0.6
- w_out: bfloat16 [768, 768], P('tensor'), may hold values from -1.75 to 1.75
- out_bias: float32 [768], replicated, may hold values from -0.6 to 0.6
- ln2_gain: float32 [768], replicated, may hold values from 0.5 to 1.5
- ln2_bias: float32 [768], replicated, may hold values from -0.6 to 0.6
- w_up: bfloat16 [2, 768, 3072], P(None, None, 'tensor'), may hold values from -0.21875 to 0.21875
- up_bias: float32 [2, 3072], P(None, 'tensor'), may hold values from -0.6 to 0.6
- w_down: bfloat16 [2, 3072, 768], P(None, 'tensor'), may hold values from -0.109375 to 0.109375
- down_bias: float32 [2, 768], replicated, may hold values from -0.6 to 0.6
Outputs:
- output: bfloat16 [7584, 768], P('dp')
- grad_tokens: bfloat16 [7584, 768], P('dp')
- grad_ln1_gain: float32 [768], replicated
- grad_ln1_bias: float32 [768], replicated
- grad_qkv: float32 [768, 3, 768], P(None, None, 'tensor')
- grad_qv_bias: float32 [2, 768], P(None, 'tensor')
- grad_out: float32 [768, 768], P('tensor')
- grad_out_bias: float32 [768], replicated
- grad_ln2_gain: float32 [768], replicated
- grad_ln2_bias: float32 [768], replicated
- grad_up: float32 [2, 768, 3072], P(None, None, 'tensor')
- grad_up_bias: float32 [2, 3072], P(None, 'tensor')
- grad_down: float32 [2, 3072, 768], P(None, 'tensor')
- grad_down_bias: float32 [2, 768], replicated
- counts: int32 [2], replicated
Inputs may be any that keep to these rules, and one draw needn't show every extreme that they name: `token_mask`: in every item of 237 rows the first 197 rows are 1; the last 40 rows hold a leading run of 1 of 8 to 40 rows where the item's expert_type is 1, and are all 0 where it is 0; the last item has a run of 40. `expert_type`: the same on all 237 rows of an item; the first item is 0 and the last is 1.
All inputs are finite; a program needn't handle non-finite values.
Results may differ from a plain program's by a relative error of at most 0.013.
Values may be sent and summed in bfloat16 or wider, within the bound.
No kernel may reach another device: no remote copies, remote signals or barrier semaphores. Data moves between devices by JAX's collectives and lax.ppermute only.
A program may use at most 128 MiB of HBM per device.

v0:
```python
import jax
import jax.numpy as jnp
from jax import lax
from jax.sharding import PartitionSpec as P

HEAD = 64
PATCHES = 197
CAP = 40


epsilon = 1e-05
highest = lax.Precision.HIGHEST


def normalize_rows(field):
    mean_row = jnp.mean(field, -1, keepdims=True)
    centered = field - mean_row
    scale_row = lax.rsqrt(jnp.mean(centered * centered, -1, keepdims=True) + epsilon)
    return (centered * scale_row, scale_row)


def norm_backward(grad_normed, unit_rows, scale_row, gain):
    grad_unit = grad_normed * gain
    return scale_row * (
        grad_unit
        - jnp.mean(grad_unit, -1, keepdims=True)
        - unit_rows * jnp.mean(grad_unit * unit_rows, -1, keepdims=True)
    )


def smooth_gate(field):
    return jax.nn.gelu(field, approximate=False)


def sum_over_items(pieces):
    flat = jnp.concatenate([piece.reshape(-1) for piece in pieces])
    share = lax.psum_scatter(flat, "dp", scatter_dimension=0, tiled=True)
    whole = lax.all_gather(share.astype(jnp.bfloat16), "dp", axis=0, tiled=True).astype(share.dtype)
    results = []
    start = 0
    for piece in pieces:
        results.append(whole[start : start + piece.size].reshape(piece.shape))
        start = start + piece.size
    return results


def local(
    tokens,
    token_mask,
    expert_type,
    cotangent,
    ln1_gain,
    ln1_bias,
    w_qkv,
    qv_bias,
    w_out,
    out_bias,
    ln2_gain,
    ln2_bias,
    w_up,
    up_bias,
    w_down,
    down_bias,
):
    row_count, feature_count = tokens.shape
    seq_length = PATCHES + CAP
    item_count = row_count // seq_length
    local_heads = w_qkv.shape[2] // HEAD
    mask_float = token_mask.astype(jnp.float32)
    language = expert_type == 1
    local_counts = jnp.stack(
        [
            jnp.sum(jnp.where(language, 0.0, mask_float)),
            jnp.sum(jnp.where(language, mask_float, 0.0)),
        ]
    )
    totals = lax.psum(local_counts, "dp")
    row_weight = (
        mask_float * (totals[0] + totals[1]) / (2.0 * jnp.where(language, totals[1], totals[0]))
    )
    expert_rows = (expert_type[:, None] == jnp.arange(2)[None, :]).astype(jnp.float32)
    item_expert = expert_type.reshape(item_count, seq_length)[:, 0]
    item_rows = (item_expert[:, None] == jnp.arange(2)[None, :]).astype(jnp.float32)
    item_language = (item_expert == 1)[:, None, None]
    up_items = jnp.where(item_language, w_up[1], w_up[0])
    down_items = jnp.where(item_language, w_down[1], w_down[0])
    up_bias_items = jnp.dot(item_rows, up_bias, precision=highest)
    down_bias_rows = jnp.dot(expert_rows, down_bias, precision=highest)
    stream = tokens.astype(jnp.float32)
    unit_one, scale_one = normalize_rows(stream)
    normed = (unit_one * ln1_gain + ln1_bias).astype(jnp.bfloat16)
    bias_three = jnp.stack([qv_bias[0], jnp.zeros_like(qv_bias[0]), qv_bias[1]])
    projected = (
        jnp.einsum("rd,dje->rje", normed, w_qkv, preferred_element_type=jnp.float32) + bias_three
    ).astype(jnp.bfloat16)
    split_heads = projected.reshape(item_count, seq_length, 3, local_heads, HEAD)
    queries = split_heads[:, :, 0]
    key_rows = split_heads[:, :, 1]
    value_rows = split_heads[:, :, 2]
    key_mask = (token_mask.reshape(item_count, seq_length) > 0)[:, None, None, :]

    def raw_scores():
        scores = (
            jnp.einsum("iqhe,ikhe->ihqk", queries, key_rows, preferred_element_type=jnp.float32)
            * 0.125
        )
        return jnp.where(key_mask, scores, -1e30)

    scores = raw_scores()
    row_max = jnp.max(scores, -1, keepdims=True)
    log_total = row_max + jnp.log(jnp.sum(jnp.exp(scores - row_max), -1, keepdims=True))
    attention = jnp.exp(scores - log_total).astype(jnp.bfloat16)
    context = (
        jnp.einsum("ihqk,ikhe->iqhe", attention, value_rows, preferred_element_type=jnp.float32)
        .astype(jnp.bfloat16)
        .reshape(row_count, local_heads * HEAD)
    )
    attn_part = jnp.dot(context, w_out, preferred_element_type=jnp.float32)
    portion = row_count // lax.axis_size("tensor")
    offset = lax.axis_index("tensor") * portion
    middle = (
        lax.dynamic_slice_in_dim(stream, offset, portion, 0)
        + lax.psum_scatter(attn_part, "tensor", scatter_dimension=0, tiled=True)
        + out_bias
    )
    unit_two, scale_two = normalize_rows(middle)
    normed_local = (unit_two * ln2_gain + ln2_bias).astype(jnp.bfloat16)
    normed_two = lax.all_gather(normed_local, "tensor", axis=0, tiled=True)
    normed_items = normed_two.reshape(item_count, seq_length, feature_count)
    hidden = (
        jnp.einsum("isd,idf->isf", normed_items, up_items, preferred_element_type=jnp.float32)
        + up_bias_items[:, None, :]
    )
    activated = smooth_gate(hidden).astype(jnp.bfloat16)
    down_part = jnp.einsum(
        "isf,ifd->isd", activated, down_items, preferred_element_type=jnp.float32
    ).reshape(row_count, feature_count)
    out_grad = cotangent.astype(jnp.float32) * row_weight[:, None]
    expert_part = lax.psum_scatter(
        down_part.astype(jnp.bfloat16), "tensor", scatter_dimension=0, tiled=True
    ).astype(jnp.float32)
    summed = middle + expert_part + lax.dynamic_slice_in_dim(down_bias_rows, offset, portion, 0)
    output = lax.all_gather(summed.astype(jnp.bfloat16), "tensor", axis=0, tiled=True)
    grad_here = lax.dynamic_slice_in_dim(out_grad, offset, portion, 0)
    grad_down_bias = jnp.dot(expert_rows.T, out_grad, precision=highest)
    grad_items = out_grad.astype(jnp.bfloat16).reshape(item_count, seq_length, feature_count)
    grad_active = jnp.einsum(
        "isd,ifd->isf", grad_items, down_items, preferred_element_type=jnp.float32
    )
    grad_down_items = jnp.einsum(
        "isf,isd->ifd", activated, grad_items, preferred_element_type=jnp.float32
    )
    gated_value, pull_gate = jax.vjp(smooth_gate, hidden)
    grad_hidden = pull_gate(grad_active)[0].astype(jnp.bfloat16)
    grad_up_items = jnp.einsum(
        "isd,isf->idf", normed_items, grad_hidden, preferred_element_type=jnp.float32
    )
    grad_up_bias = jnp.einsum(
        "ie,if->ef", item_rows, jnp.sum(grad_hidden.astype(jnp.float32), 1), precision=highest
    )
    grad_up = jnp.einsum("ie,idf->edf", item_rows, grad_up_items, precision=highest)
    grad_down = jnp.einsum("ie,ifd->efd", item_rows, grad_down_items, precision=highest)
    norm_two_part = jnp.einsum(
        "isf,idf->isd", grad_hidden, up_items, preferred_element_type=jnp.float32
    ).reshape(row_count, feature_count)
    grad_norm_two = lax.psum_scatter(norm_two_part, "tensor", scatter_dimension=0, tiled=True)
    grad_ln2_gain = jnp.sum(grad_norm_two * unit_two, 0)
    grad_ln2_bias = jnp.sum(grad_norm_two, 0)
    grad_middle = grad_here + norm_backward(grad_norm_two, unit_two, scale_two, ln2_gain)
    grad_out_bias = jnp.sum(grad_middle, 0)
    branch_local = grad_middle.astype(jnp.bfloat16)
    grad_branch = lax.all_gather(branch_local, "tensor", axis=0, tiled=True)
    grad_out = jnp.dot(context.T, grad_branch, preferred_element_type=jnp.float32)
    grad_context = (
        jnp.dot(grad_branch, w_out.T, preferred_element_type=jnp.float32)
        .astype(jnp.bfloat16)
        .reshape(item_count, seq_length, local_heads, HEAD)
    )
    scores_again = raw_scores()
    attention_full = jnp.exp(scores_again - log_total)
    attention_low = attention_full.astype(jnp.bfloat16)
    grad_attention = jnp.einsum(
        "iqhe,ikhe->ihqk", grad_context, value_rows, preferred_element_type=jnp.float32
    )
    grad_values = jnp.einsum(
        "ihqk,iqhe->ikhe", attention_low, grad_context, preferred_element_type=jnp.float32
    )
    grad_scores = (
        attention_full
        * (grad_attention - jnp.sum(grad_attention * attention_full, -1, keepdims=True))
    ).astype(jnp.bfloat16)
    grad_queries = (
        jnp.einsum("ihqk,ikhe->iqhe", grad_scores, key_rows, preferred_element_type=jnp.float32)
        * 0.125
    )
    grad_keys = (
        jnp.einsum("ihqk,iqhe->ikhe", grad_scores, queries, preferred_element_type=jnp.float32)
        * 0.125
    )
    grad_projected = (
        jnp.stack([grad_queries, grad_keys, grad_values], 2)
        .astype(jnp.bfloat16)
        .reshape(row_count, 3, local_heads * HEAD)
    )
    grad_projected_float = grad_projected.astype(jnp.float32)
    grad_qv_bias = jnp.stack(
        [jnp.sum(grad_projected_float[:, 0], 0), jnp.sum(grad_projected_float[:, 2], 0)]
    )
    grad_qkv = jnp.einsum("rd,rje->dje", normed, grad_projected, preferred_element_type=jnp.float32)
    norm_one_part = jnp.einsum(
        "rje,dje->rd", grad_projected, w_qkv, preferred_element_type=jnp.float32
    )
    grad_norm_one = lax.psum_scatter(norm_one_part, "tensor", scatter_dimension=0, tiled=True)
    unit_here = lax.dynamic_slice_in_dim(unit_one, offset, portion, 0)
    scale_here = lax.dynamic_slice_in_dim(scale_one, offset, portion, 0)
    grad_ln1_gain = jnp.sum(grad_norm_one * unit_here, 0)
    grad_ln1_bias = jnp.sum(grad_norm_one, 0)
    grad_input = (
        grad_middle + norm_backward(grad_norm_one, unit_here, scale_here, ln1_gain)
    ).astype(jnp.bfloat16)
    grad_tokens = lax.all_gather(grad_input, "tensor", axis=0, tiled=True)
    grad_ln1_gain, grad_ln1_bias, grad_out_bias, grad_ln2_gain, grad_ln2_bias = lax.psum(
        (grad_ln1_gain, grad_ln1_bias, grad_out_bias, grad_ln2_gain, grad_ln2_bias),
        ("dp", "tensor"),
    )
    grad_qkv, grad_qv_bias, grad_out, grad_up, grad_up_bias, grad_down, grad_down_bias = (
        sum_over_items(
            [grad_qkv, grad_qv_bias, grad_out, grad_up, grad_up_bias, grad_down, grad_down_bias]
        )
    )
    counts = totals.astype(jnp.int32)
    return (
        output,
        grad_tokens,
        grad_ln1_gain,
        grad_ln1_bias,
        grad_qkv,
        grad_qv_bias,
        grad_out,
        grad_out_bias,
        grad_ln2_gain,
        grad_ln2_bias,
        grad_up,
        grad_up_bias,
        grad_down,
        grad_down_bias,
        counts,
    )


def solution(mesh):
    in_specs = (
        P("dp", None),
        P("dp"),
        P("dp"),
        P("dp", None),
        P(),
        P(),
        P(None, None, "tensor"),
        P(None, "tensor"),
        P("tensor", None),
        P(),
        P(),
        P(),
        P(None, None, "tensor"),
        P(None, "tensor"),
        P(None, "tensor", None),
        P(),
    )
    out_specs = (
        P("dp", None),
        P("dp", None),
        P(),
        P(),
        P(None, None, "tensor"),
        P(None, "tensor"),
        P("tensor", None),
        P(),
        P(),
        P(),
        P(None, None, "tensor"),
        P(None, "tensor"),
        P(None, "tensor", None),
        P(),
        P(),
    )
    return jax.shard_map(local, mesh=mesh, in_specs=in_specs, out_specs=out_specs, check_vma=False)
```

profile of v0, /device:TPU:0, one launch (start us, length us, event | category | flops | bytes accessed | tf_op | source)
XLA Modules:
  0.0 1170.3 jit_solution(7838384029867181379)
XLA Ops:
  25.3 31.9 %fusion = f32[240,768]{1,0:T(8,128)S(1)} fusion(f32[948,768]{1,0:T(8,128)} %fusion.88), kind=kCustom, calls=%all-reduce-scatter | all-reduce-scatter fusion | flops 737281 | bytes 3650048
  62.2 22.3 %psum.42 = f32[2]{0:T(128)} all-reduce(f32[2]{0:T(128)} %pad_maximum_fusion.2), channel_id=1, replica_groups=mesh['dp'=8,'tensor'=4] {'dp'}, use_global_device_ids=true, to_apply=%region_10.11 | all-reduce | flops 2 | bytes 16 | tf_op jit(solution)/shard_map/psum | solution.py:77
  121.3 7.6 multiply_convert_fusion.1
  135.4 18.3 %fusion.1 = bf16[240,768]{1,0:T(8,128)(2,1)} fusion(bf16[948,768]{1,0:T(8,128)(2,1)} %convert_element_type.89), kind=kCustom, calls=%all-reduce-scatter.1 | all-reduce-scatter fusion | flops 737281 | bytes 1825280
  156.9 6.0 convert_reduce_fusion
  170.9 31.5 %fusion.2 = f32[240,768]{1,0:T(8,128)} fusion(f32[948,768]{1,0:T(8,128)} %reshape.209), kind=kCustom, calls=%all-reduce-scatter.2 | all-reduce-scatter fusion | flops 737281 | bytes 3650048
  213.5 4.6 concatenate.7
  231.7 12.1 %fusion.6 = f32[2,768,768]{2,0,1:T(2,128)S(1)} fusion(f32[4,768,768]{2,1,0:T(8,128)S(1)} %fusion.90, s32[4]{0:T(128)S(1)} %copy-done.40), kind=kOutput, calls=%fused_computation.2 | convolution fusion | flops 56623112 | bytes 14155792 | tf_op jit(solution)/shard_map/ie,idf->edf/dot_general | solution.py:161
  246.4 5.7 reshape.214
  255.5 12.1 %fusion.4 = f32[2,768,768]{2,0,1:T(2,128)S(1)} fusion(f32[4,768,768]{2,1,0:T(8,128)S(1)} %fusion.91, s32[4]{0:T(128)S(1)} %copy-done.40), kind=kOutput, calls=%fused_computation | convolution fusion | flops 56623112 | bytes 14155792 | tf_op jit(solution)/shard_map/ie,ifd->efd/dot_general | solution.py:162
  270.2 5.7 reshape.216
  314.6 4.7 reshape.211
  322.1 30.8 %fusion.3 = f32[240,768]{1,0:T(8,128)S(1)} fusion(f32[948,768]{1,0:T(8,128)} %convolution_bitcast_fusion), kind=kCustom, calls=%all-reduce-scatter.3 | all-reduce-scatter fusion | flops 737281 | bytes 3650048
  362.3 40.8 %dynamic-update-slice.4 = f32[2952576]{0:T(1024)} dynamic-update-slice(f32[2952576]{0:T(1024)} %constant_dynamic-update-slice_fusion.6, f32[1179648]{0:T(1024)} %reshape.214, s32[]{} %constant.134) | dynamic-update-slice | bytes 9437188
  404.5 40.8 %dynamic-update-slice.6 = f32[2952576]{0:T(1024)} dynamic-update-slice(f32[2952576]{0:T(1024)} %constant_dynamic-update-slice_fusion.5, f32[1179648]{0:T(1024)} %reshape.216, s32[]{} %constant.136) | dynamic-update-slice | bytes 9437188
  452.7 458.9 %all-reduce.15 = bf16[2952576]{0:T(1024)(128)(2,1)} all-reduce(f32[2952576]{0:T(1024)} %constant_dynamic-update-slice_fusion.4), channel_id=6, replica_groups=mesh['dp'=8,'tensor'=4] {'dp'}, use_global_device_ids=true, to_apply=%region_25.26.clone | all-reduce | flops 2952576 | bytes 17715456
  915.9 12.0 %dynamic-update-slice = bf16[2952576]{0:T(1024)(128)(2,1)} dynamic-update-slice(bf16[2952576]{0:T(1024)(128)(2,1)} %broadcast.235, bf16[369072]{0:T(1024)(128)(2,1)S(1)} %dynamic-slice.48, u32[]{:T(128)} %bitcast.27) | dynamic-update-slice | bytes 1476292
  932.0 42.2 %all-reduce.10 = (f32[768]{0:T(1024)}, f32[768]{0:T(1024)}, f32[768]{0:T(1024)}, f32[768]{0:T(1024)}, f32[768]{0:T(1024)}) all-reduce(f32[768]{0:T(1024)S(1)} %get-tuple-element.60, f32[768]{0:T(1024)S(1)} %get-tuple-element.71, f32[768]{0:T(1024)S(1)} %get-tuple-element.79, ...), channel_id=1, replica_groups=mesh['dp'=8,'tensor'=4] {'dp','tensor'}, use_global_device_ids=true, to_apply=%region_19.20 | all-reduce | flops 3840 | bytes 30720 | tf_op jit(solution)/shard_map/psum | solution.py:222
  977.1 152.2 %all-reduce.14.cloned.1.call-done = bf16[2952576]{0:T(1024)(128)(2,1)} async-done(((bf16[2952576]{0:T(1024)(128)(2,1)}), bf16[2952576]{0:T(1024)(128)(2,1)}) %all-reduce.14.cloned.1.call-update) | async-done | bytes 5905168
  1129.2 5.8 fusion.83
  1135.0 6.0 reshape.219
  1141.0 6.0 reshape.221
  1149.4 4.7 slice.100
  1154.1 4.2 copy.94
  (237 shorter events, 185.5 us)
Async XLA Ops:
  7.2 109.8 %all-gather.9.cloned.1.call-start = ((), (), s32[]{:S(2)}) async-start(), calls=%async_computation.1 | async-start | bytes 1843200 | tf_op jit(solution)/shard_map/all_gather | solution.py:128
  23.1 34.7 %copy-start.26 = (s32[948]{0:T(1024)S(1)}, s32[948]{0:T(1024)}, u32[]{:S(2)}) copy-start(s32[948]{0:T(1024)} %param.18) | copy-start | bytes 11380
  60.9 33.1 %collective-permute-start = (f32[9,768]{1,0:T(8,128)}, f32[9,768]{1,0:T(8,128)S(1)}, u32[]{:S(2)}, u32[]{:S(2)}) collective-permute-start(f32[9,768]{1,0:T(8,128)} %slice.121), channel_id=1, source_target_pairs={{0,1},{1,2},{2,3},{4,5},{5,6},{6,7},{8,9},{9,10},{10,11},{12,13},{... | collective-permute-start | bytes 82952
  91.5 7.9 copy-start.25
  99.1 5.3 copy-start.29
  100.4 7.2 copy-start.42
  100.4 7.3 copy-start.44
  100.4 7.5 copy-start.43
  100.4 175.8 %all-gather.13.cloned.1.call-start = ((), (), s32[]{:S(2)}) async-start(), calls=%async_computation.3 | async-start | bytes 1843200 | tf_op jit(solution)/shard_map/all_gather | solution.py:172
  121.2 7.6 copy-start.12
  121.2 8.7 copy-start.21
  121.3 8.7 copy-start.22
  155.0 58.5 %collective-permute-start.1 = (bf16[9,768]{1,0:T(8,128)(2,1)}, bf16[9,768]{1,0:T(8,128)(2,1)}, u32[]{:S(2)}, u32[]{:S(2)}) collective-permute-start(bf16[9,768]{1,0:T(8,128)(2,1)} %slice.122), channel_id=1, source_target_pairs={{0,1},{1,2},{2,3},{4,5},{5,6},{6,7},{8,9},{9,10},{10,11},{12,13},{... | collective-permute-start | bytes 41480
  156.9 7.2 copy-start.19
  156.9 7.2 copy-start.20
  203.9 14.3 %collective-permute-start.2 = (f32[9,768]{1,0:T(8,128)}, f32[9,768]{1,0:T(8,128)S(1)}, u32[]{:S(2)}, u32[]{:S(2)}) collective-permute-start(f32[9,768]{1,0:T(8,128)} %slice.123), channel_id=1, source_target_pairs={{0,1},{1,2},{2,3},{4,5},{5,6},{6,7},{8,9},{9,10},{10,11},{12,13},{... | collective-permute-start | bytes 82952
  228.4 700.8 %all-gather.11.cloned.1.call-start = ((), (), s32[]{:S(2)}) async-start(), calls=%async_computation.2 | async-start | bytes 1843200 | tf_op jit(solution)/shard_map/all_gather | solution.py:143
  246.4 5.7 copy-start.41
  276.0 8.1 copy-start.31
  276.0 698.2 %all-gather.15.cloned.1.call-start = ((), (), s32[]{:S(2)}) async-start(), calls=%async_computation.4 | async-start | bytes 1843200 | tf_op jit(solution)/shard_map/all_gather | solution.py:221
  281.9 5.4 copy-start.17
  357.6 89.1 %collective-permute-start.3 = (f32[9,768]{1,0:T(8,128)S(1)}, f32[9,768]{1,0:T(8,128)S(1)}, u32[]{:S(2)}, u32[]{:S(2)}) collective-permute-start(f32[9,768]{1,0:T(8,128)S(1)} %slice.124), channel_id=1, source_target_pairs={{0,1},{1,2},{2,3},{4,5},{5,6},{6,7},{8,9},{9,10},{10,11},{12,13},{... | collective-permute-start | bytes 82952
  404.5 40.8 %copy-start.28 = (f32[1536]{0:T(1024)S(1)}, f32[1536]{0:T(1024)}, u32[]{:S(2)}) copy-start(f32[1536]{0:T(1024)} %reshape.217) | copy-start | bytes 18436
  452.7 676.6 %all-reduce.14.cloned.1.call-start = ((), (), s32[]{:S(2)}) async-start(), calls=%async_computation | async-start | bytes 11812864
  (35 other events, 99.9 us)
Sparse Core Ops, SparseCore 0:
  100.5 16.0 all-gather.8
  228.5 20.0 all-gather.12
  276.1 20.0 all-gather.10
  452.8 20.2 all-gather.14
  928.1 201.0 all-reduce.13
where the time goes:
time: 1190 us; the launch traced here: 1170 us
  blocking collectives  636 us (53%)
  local copies, waits for them, and re-layouts  239 us (20%)
  waiting for transfers between devices  152 us (13%)
  matrix products  76.2 us (6%)
  other arithmetic  41.9 us (4%)
  between operations  18 us (2%)
    unnamed x5, blocking collectives  571 us
    unnamed x10, waiting for transfers between devices  152 us
    unnamed x125, local copies, waits for them, and re-layouts  145 us
    psum x1, blocking collectives, local(): lax.psum((grad_ln1_gain, grad_ln1_bias, grad_out_bias, grad_ln2_gain, gra...  42.2 us
  transfers between devices with their start and end apart: 9, of which 1 were waited for; matrix products, arithmetic and copies ran while one was open for 28% of the time, Pallas kernels for 0%

commit v1 on v0

v1 whole, which is shorter than its diff:
```python
import functools

import jax
import jax.numpy as jnp
from jax import lax
from jax.experimental import pallas as pl
from jax.experimental.pallas import tpu as pltpu
from jax.sharding import PartitionSpec as P

HEAD = 64
PATCHES = 197
CAP = 40
SEQ = PATCHES + CAP
PAD = 240
ATT = 256

epsilon = 1e-05
f32 = jnp.float32
bf16 = jnp.bfloat16

NT = (((1,), (1,)), ((), ()))
NN = (((1,), (0,)), ((), ()))
TN = (((0,), (0,)), ((), ()))


def dot(a, b, dims=NN):
    return lax.dot_general(a, b, dims, preferred_element_type=f32)


def iota(shape, dim):
    return lax.broadcasted_iota(jnp.int32, shape, dim)


def unit_rows(x):
    mean = jnp.mean(x, -1, keepdims=True)
    centered = x - mean
    scale = lax.rsqrt(jnp.mean(centered * centered, -1, keepdims=True) + epsilon)
    return centered * scale, scale


def norm_back(grad, unit, scale, gain):
    t = grad * gain
    return scale * (
        t - jnp.mean(t, -1, keepdims=True) - unit * jnp.mean(t * unit, -1, keepdims=True)
    )


VMEM = pltpu.VMEM
SMEM = pltpu.SMEM


def vspec():
    return pl.BlockSpec(memory_space=VMEM)


def sspec():
    return pl.BlockSpec(memory_space=SMEM)


def aspec():
    return pl.BlockSpec(memory_space=pl.ANY)


def call(kernel, ins, specs, outs, scratch=(), limit=40, flops=0, name=None):
    size = sum(a.size * a.dtype.itemsize for a in ins)
    size += sum(o.size * o.dtype.itemsize for o in outs)
    return pl.pallas_call(
        kernel,
        out_shape=list(outs),
        in_specs=list(specs),
        out_specs=[vspec() for _ in outs],
        scratch_shapes=list(scratch),
        compiler_params=pltpu.CompilerParams(vmem_limit_bytes=limit * 1024 * 1024),
        cost_estimate=pl.CostEstimate(
            flops=int(flops), bytes_accessed=int(size), transcendentals=0
        ),
        name=name,
    )(*ins)


def arr(shape, dtype):
    return jax.ShapeDtypeStruct(shape, dtype)


def stage_rows(ref, buf, chunk):
    low = 2 * chunk * SEQ
    high = low + 2 * SEQ
    base = low // 16 * 16
    top = min(ref.shape[0], -(-high // 16) * 16)
    buf[0 : top - base] = ref[...][base:top].astype(f32)
    return [low - base, low - base + SEQ]


def item_rows(buf, offset, count):
    rows = buf[pl.ds(offset, count), :]
    return jnp.where(iota(rows.shape, 0) < SEQ, rows, 0.0)


STAGE = 2 * SEQ + 32


def attention_forward(chunk, items, heads, meta, tokens, w_t, b_three, gain, bias, ctx, proj, normed, buf):
    width = heads * HEAD
    offsets = stage_rows(tokens, buf, chunk)
    for j in range(2):
        live = meta[1 + 2 * chunk + j]
        x = item_rows(buf, offsets[j], ATT)
        unit, _ = unit_rows(x)
        n_row = (unit * gain[...] + bias[...]).astype(bf16)
        normed[j] = n_row[:PAD]
        p_row = (dot(n_row, w_t[...], NT) + b_three[...]).astype(bf16)
        proj[j] = p_row[:PAD]
        key_live = iota((ATT, ATT), 1) < live
        for h in range(heads):
            q = p_row[:, h * HEAD : (h + 1) * HEAD]
            k = p_row[:, width + h * HEAD : width + (h + 1) * HEAD]
            v = p_row[:, 2 * width + h * HEAD : 2 * width + (h + 1) * HEAD]
            s = jnp.where(key_live, dot(q, k, NT) * 0.125, -1e30)
            e = jnp.exp(s - jnp.max(s, -1, keepdims=True))
            att = (e * (1.0 / jnp.sum(e, -1, keepdims=True))).astype(bf16)
            c = dot(att, v).astype(bf16)
            at = j * width + h * HEAD
            ctx[:, at : at + HEAD] = c[:PAD]


def run_attention_forward(chunk, items, heads, meta, tokens, w_t, b_three, gain, bias):
    width = heads * HEAD
    d = tokens.shape[1]
    return call(
        functools.partial(attention_forward, chunk, items, heads),
        (meta, tokens, w_t, b_three, gain, bias),
        [sspec()] + [vspec()] * 5,
        [arr((PAD, 2 * width), bf16), arr((2, PAD, 3 * width), bf16), arr((2, PAD, d), bf16)],
        [VMEM((STAGE, d), f32)],
        flops=2 * 2 * ATT * (d * 3 * width + 4 * ATT * width),
        name="attention_forward_%d" % chunk,
    )


def gelu_parts(h):
    cdf = 0.5 * (1.0 + lax.erf(h * 0.7071067811865476))
    density = jnp.exp(-0.5 * h * h) * 0.3989422804014327
    return h * cdf, cdf + h * density


def experts(
    chunk, items, heads, meta, weight, tokens, cot, c0, c1, c2, c3, o0, o1, o2, o3, out_bias, gain, bias,
    up_bias, w_up_any, w_down_any,
    middle, own_grad, normed, active, ghid, gout, down_own, down_other, part_own, part_other, small,
    buf, cbuf, ctx, w_out, w_up, w_down, sems,
):
    width = heads * HEAD
    copy_up = pltpu.make_async_copy(w_up_any, w_up, sems.at[0])
    copy_down = pltpu.make_async_copy(w_down_any, w_down, sems.at[1])
    copy_up.start()
    copy_down.start()
    t = meta[0]
    core = lax.rem(t, 2)
    first = core == 0
    for step, (c, o) in enumerate(((c0, o0), (c1, o1), (c2, o2), (c3, o3))):
        if step == 0:
            slot = t
        elif step == 1:
            slot = t + 1 - 2 * core
        elif step == 2:
            slot = lax.rem(t + 2, 4)
        else:
            slot = lax.rem(t + 3 - 2 * core, 4)
        ctx[slot] = c[...]
        w_out[slot] = o[...]
    offsets = stage_rows(tokens, buf, chunk)
    cot_offsets = stage_rows(cot, cbuf, chunk)
    mids, grads, n_rows = [], [], []
    for j in range(2):
        x = item_rows(buf, offsets[j], PAD)
        total = jnp.zeros((PAD, x.shape[1]), f32)
        for s in range(4):
            total = total + dot(ctx[s][:, j * width : (j + 1) * width], w_out[s])
        mid = x + total + out_bias[...]
        mids.append(mid)
        unit, _ = unit_rows(mid)
        n_row = (unit * gain[...] + bias[...]).astype(bf16)
        normed[j] = n_row
        n_rows.append(n_row)
        raw = item_rows(cbuf, cot_offsets[j], PAD)
        live = iota(raw.shape, 0) < meta[1 + 2 * chunk + j]
        grad = jnp.where(live, raw, 0.0) * weight[2 * chunk + j]
        grads.append(grad)
        gout[j] = grad.astype(bf16)
    middle[...] = jnp.where(first, mids[0], mids[1])
    own_grad[...] = jnp.where(first, grads[0], grads[1])
    small[...] = jnp.zeros_like(small)
    copy_up.wait()
    copy_down.wait()
    parts, downs = [], []
    for j in range(2):
        e = meta[1 + items + 2 * chunk + j]
        wu = w_up[e]
        wd = w_down[e]
        h = dot(n_rows[j], wu) + up_bias[e]
        value, slope = gelu_parts(h)
        act = value.astype(bf16)
        active[j] = act
        gh = (dot(gout[j], wd, NT) * slope).astype(bf16)
        ghid[j] = gh
        part = dot(gh, wu, NT)
        parts.append(part)
        downs.append(dot(act, wd))
        small[pl.ds(e, 1), :] += jnp.sum(gh.astype(f32), 0, keepdims=True)
        small[pl.ds(e + 2, 1), :] += jnp.sum(grads[j], 0, keepdims=True)
    part_own[...] = jnp.where(first, parts[0], parts[1]).astype(bf16)
    part_other[...] = jnp.where(first, parts[1], parts[0]).astype(bf16)
    down_own[...] = jnp.where(first, downs[0], downs[1]).astype(bf16)
    down_other[...] = jnp.where(first, downs[1], downs[0]).astype(bf16)


def run_experts(chunk, items, heads, meta, weight, tokens, cot, ctxs, outs, out_bias, gain, bias, up_bias, w_up, w_down):
    width = heads * HEAD
    d = tokens.shape[1]
    ff = w_up.shape[2]
    row = arr((PAD, d), bf16)
    return call(
        functools.partial(experts, chunk, items, heads),
        (meta, weight, tokens, cot, *ctxs, *outs, out_bias, gain, bias, up_bias, w_up, w_down),
        [sspec()] * 2 + [vspec()] * 14 + [aspec()] * 2,
        [
            arr((PAD, d), f32),
            arr((PAD, d), f32),
            arr((2, PAD, d), bf16),
            arr((2, PAD, ff), bf16),
            arr((2, PAD, ff), bf16),
            arr((2, PAD, d), bf16),
            row,
            row,
            row,
            row,
            arr((8, d), f32),
        ],
        [
            VMEM((STAGE, d), f32),
            VMEM((STAGE, d), f32),
            VMEM((4, PAD, 2 * width), bf16),
            VMEM((4, width, d), bf16),
            VMEM(w_up.shape, bf16),
            VMEM(w_down.shape, bf16),
            pltpu.SemaphoreType.DMA((2,)),
        ],
        flops=2 * 2 * PAD * d * (4 * width + 4 * ff),
        limit=48,
        name="experts_%d" % chunk,
    )


def expert_grads(items, meta, *refs):
    lefts, rights = refs[: items // 2], refs[items // 2 : items]
    out, total = refs[items], refs[items + 1]
    total[...] = jnp.zeros_like(total)
    for i in range(items):
        e = meta[1 + items + i]
        total[e] += dot(lefts[i // 2][i % 2], rights[i // 2][i % 2], TN)
    out[...] = total[...].astype(bf16)


def run_expert_grads(items, meta, lefts, rights, name):
    shape = (2, lefts[0].shape[2], rights[0].shape[2])
    return call(
        functools.partial(expert_grads, items),
        (meta, *lefts, *rights),
        [sspec()] + [vspec()] * items,
        [arr(shape, bf16)],
        [VMEM(shape, f32)],
        flops=2 * items * PAD * shape[1] * shape[2],
        name=name,
    )[0]


def norm_two_back(middle, own_grad, pair, far, gain, grad_mid, branch, small):
    unit, scale = unit_rows(middle[...])
    grad = pair[...].astype(f32) + far[...].astype(f32)
    out = own_grad[...] + norm_back(grad, unit, scale, gain[...])
    grad_mid[...] = out
    branch[...] = out.astype(bf16)
    small[...] = jnp.zeros_like(small)
    small[0:1, :] = jnp.sum(grad * unit, 0, keepdims=True)
    small[1:2, :] = jnp.sum(grad, 0, keepdims=True)
    small[2:3, :] = jnp.sum(out, 0, keepdims=True)


def run_norm_two_back(chunk, middle, own_grad, pair, far, gain):
    shape = middle.shape
    return call(
        norm_two_back,
        (middle, own_grad, pair, far, gain),
        [vspec()] * 5,
        [arr(shape, f32), arr(shape, bf16), arr((8, shape[1]), f32)],
        flops=20 * middle.size,
        name="norm_two_back_%d" % chunk,
    )


def attention_backward(chunk, items, heads, meta, own, other, w_out, proj, w_t, gproj, part_own, part_other, small):
    width = heads * HEAD
    first = lax.rem(meta[0], 2) == 0
    parts = []
    small[...] = jnp.zeros_like(small)
    for j in range(2):
        live = meta[1 + 2 * chunk + j]
        a, b = (own, other) if j == 0 else (other, own)
        branch = jnp.where(first, a[...], b[...])
        gctx = dot(branch, w_out[...], NT).astype(bf16)
        p_row = proj[j]
        key_live = iota((PAD, PAD), 1) < live
        gq, gk, gv = [], [], []
        for h in range(heads):
            q = p_row[:, h * HEAD : (h + 1) * HEAD]
            k = p_row[:, width + h * HEAD : width + (h + 1) * HEAD]
            v = p_row[:, 2 * width + h * HEAD : 2 * width + (h + 1) * HEAD]
            gc = gctx[:, h * HEAD : (h + 1) * HEAD]
            s = jnp.where(key_live, dot(q, k, NT) * 0.125, -1e30)
            e = jnp.exp(s - jnp.max(s, -1, keepdims=True))
            att = e * (1.0 / jnp.sum(e, -1, keepdims=True))
            ga = dot(gc, v, NT)
            gs = (att * (ga - jnp.sum(ga * att, -1, keepdims=True))).astype(bf16)
            gv.append(dot(att.astype(bf16), gc, TN))
            gq.append(dot(gs, k) * 0.125)
            gk.append(dot(gs, q, TN) * 0.125)
        gp = jnp.concatenate(gq + gk + gv, axis=1).astype(bf16)
        gproj[j] = gp
        small[0:1, :] += jnp.sum(gp.astype(f32), 0, keepdims=True)
        parts.append(dot(gp, w_t[...]))
    part_own[...] = jnp.where(first, parts[0], parts[1]).astype(bf16)
    part_other[...] = jnp.where(first, parts[1], parts[0]).astype(bf16)


def run_attention_backward(chunk, items, heads, meta, own, other, w_out, proj, w_t):
    width = heads * HEAD
    d = own.shape[1]
    return call(
        functools.partial(attention_backward, chunk, items, heads),
        (meta, own, other, w_out, proj, w_t),
        [sspec()] + [vspec()] * 5,
        [arr((2, PAD, 3 * width), bf16), arr((PAD, d), bf16), arr((PAD, d), bf16), arr((8, 3 * width), f32)],
        flops=2 * 2 * PAD * (d * 4 * width + 5 * PAD * width),
        name="attention_backward_%d" % chunk,
    )


def attention_grads(items, heads, meta, *refs):
    width = heads * HEAD
    chunks = items // 2
    gproj, normed, ctx = refs[:chunks], refs[chunks : 2 * chunks], refs[2 * chunks : 3 * chunks]
    own, other = refs[3 * chunks : 4 * chunks], refs[4 * chunks : 5 * chunks]
    out = refs[5 * chunks]
    first = lax.rem(meta[0], 2) == 0
    rows = 3 * width
    total = jnp.zeros((rows, out.shape[1]), f32)
    total_out = jnp.zeros((width, out.shape[1]), f32)
    for k in range(chunks):
        for j in range(2):
            total = total + dot(gproj[k][j], normed[k][j], TN)
            a, b = (own[k], other[k]) if j == 0 else (other[k], own[k])
            branch = jnp.where(first, a[...], b[...])
            total_out = total_out + dot(ctx[k][:, j * width : (j + 1) * width], branch, TN)
    out[0:rows, :] = total.astype(bf16)
    out[rows:, :] = total_out.astype(bf16)


def run_attention_grads(items, heads, meta, gproj, normed, ctx, own, other):
    width = heads * HEAD
    d = own[0].shape[1]
    return call(
        functools.partial(attention_grads, items, heads),
        (meta, *gproj, *normed, *ctx, *own, *other),
        [sspec()] + [vspec()] * (5 * items // 2),
        [arr((4 * width, d), bf16)],
        flops=2 * items * PAD * d * 4 * width,
        name="attention_grads",
    )[0]


def norm_one_back(chunk, meta, tokens, grad_mid, pair, far, gain, grad_own, small, buf):
    first = lax.rem(meta[0], 2) == 0
    offsets = stage_rows(tokens, buf, chunk)
    x = jnp.where(first, item_rows(buf, offsets[0], PAD), item_rows(buf, offsets[1], PAD))
    unit, scale = unit_rows(x)
    grad = pair[...].astype(f32) + far[...].astype(f32)
    grad_own[...] = (grad_mid[...] + norm_back(grad, unit, scale, gain[...])).astype(bf16)
    small[...] = jnp.zeros_like(small)
    small[0:1, :] = jnp.sum(grad * unit, 0, keepdims=True)
    small[1:2, :] = jnp.sum(grad, 0, keepdims=True)


def run_norm_one_back(chunk, meta, tokens, grad_mid, pair, far, gain):
    shape = grad_mid.shape
    return call(
        functools.partial(norm_one_back, chunk),
        (meta, tokens, grad_mid, pair, far, gain),
        [sspec()] + [vspec()] * 5,
        [arr(shape, bf16), arr((8, shape[1]), f32)],
        [VMEM((STAGE, shape[1]), f32)],
        flops=20 * grad_mid.size,
        name="norm_one_back_%d" % chunk,
    )


def output_rows(chunk, items, meta, middle, pair, far, down_bias, out):
    e0 = meta[1 + items + 2 * chunk]
    e1 = meta[1 + items + 2 * chunk + 1]
    e = jnp.where(lax.rem(meta[0], 2) == 0, e0, e1)
    out[...] = (middle[...] + pair[...].astype(f32) + far[...].astype(f32) + down_bias[e]).astype(bf16)


def run_output_rows(chunk, items, meta, middle, pair, far, down_bias):
    return call(
        functools.partial(output_rows, chunk, items),
        (meta, middle, pair, far, down_bias),
        [sspec()] + [vspec()] * 4,
        [arr(middle.shape, bf16)],
        flops=4 * middle.size,
        name="output_rows_%d" % chunk,
    )[0]


def assemble(items, meta, *refs):
    chunks = items // 2
    own, other, out, buf = refs[:chunks], refs[chunks : 2 * chunks], refs[2 * chunks], refs[2 * chunks + 1]
    first = lax.rem(meta[0], 2) == 0
    for k in range(chunks):
        for j in range(2):
            a, b = (own[k], other[k]) if j == 0 else (other[k], own[k])
            rows = jnp.where(first, a[...], b[...]).astype(f32)
            buf[pl.ds((2 * k + j) * SEQ, PAD), :] = rows
    out[...] = buf[0 : items * SEQ, :].astype(bf16)


def run_assemble(items, meta, own, other, name):
    d = own[0].shape[1]
    return call(
        functools.partial(assemble, items),
        (meta, *own, *other),
        [sspec()] + [vspec()] * items,
        [arr((items * SEQ, d), bf16)],
        [VMEM((items * SEQ + 16, d), f32)],
        name=name,
    )[0]


def swap(value, axis, size, bit):
    return lax.ppermute(value, axis, [(i, i ^ bit) for i in range(size)])


def sum_over(value, axis, size):
    bit = 1
    while bit < size:
        value = value + swap(value, axis, size, bit)
        bit = 2 * bit
    return value


def sum_over_items(piece, dp):
    flat = piece.reshape(-1, piece.shape[-1])
    share = lax.psum_scatter(flat, "dp", scatter_dimension=0, tiled=True)
    return lax.all_gather(share, "dp", axis=0, tiled=True).reshape(piece.shape).astype(f32)


def local(
    dp, tp,
    tokens, token_mask, expert_type, cotangent, ln1_gain, ln1_bias, w_qkv, qv_bias, w_out, out_bias,
    ln2_gain, ln2_bias, w_up, up_bias, w_down, down_bias,
):
    rows, d = tokens.shape
    items = rows // SEQ
    width = w_qkv.shape[2]
    heads = width // HEAD
    t = lax.axis_index("tensor").astype(jnp.int32)
    core_swap = lambda v: swap(v, "tensor", tp, 1)
    far_swap = lambda v: swap(v, "tensor", tp, 2)

    lives = jnp.sum(token_mask.reshape(items, SEQ), 1)
    kinds = expert_type.reshape(items, SEQ)[:, 0]
    meta = jnp.concatenate([t[None], lives, kinds, jnp.zeros((15 - 2 * items,), jnp.int32)])
    ones = jnp.sum(jnp.where(kinds == 1, lives, 0))
    local_counts = jnp.stack([jnp.sum(lives) - ones, ones]).astype(f32)

    w_t = w_qkv.transpose(1, 2, 0).reshape(3 * width, d)
    b_three = jnp.concatenate([qv_bias[0], jnp.zeros_like(qv_bias[0]), qv_bias[1]])[None]
    row = lambda v: v.reshape(1, -1)
    up_bias3 = up_bias[:, None, :]
    down_bias3 = down_bias[:, None, :]

    o0 = w_out
    o2 = far_swap(o0)
    o1 = core_swap(o0)
    o3 = core_swap(o2)
    outs = (o0, o1, o2, o3)

    chunks = range(items // 2)
    ctx, proj, normed_one, ctxs = [], [], [], []
    for k in chunks:
        c0, p, n = run_attention_forward(k, items, heads, meta, tokens, w_t, b_three, row(ln1_gain), row(ln1_bias))
        ctx.append(c0)
        proj.append(p)
        normed_one.append(n)
        c2 = far_swap(c0)
        c1 = core_swap(c0)
        c3 = core_swap(c2)
        ctxs.append((c0, c1, c2, c3))

    totals = sum_over(local_counts, "dp", dp)
    weight = (totals[0] + totals[1]) / (2.0 * jnp.where(kinds == 1, totals[1], totals[0]))

    exp = [
        run_experts(
            k, items, heads, meta, weight, tokens, cotangent, ctxs[k], outs, row(out_bias), row(ln2_gain),
            row(ln2_bias), up_bias3, w_up, w_down,
        )
        for k in chunks
    ]
    middle, own_grad, normed_two, active, ghid, gout, down_own, down_other, part_own, part_other, small_e = zip(*exp)

    grad_down_part = run_expert_grads(items, meta, active, gout, "down_grads")
    grad_up_part = run_expert_grads(items, meta, normed_two, ghid, "up_grads")

    def pair_sum(own, other):
        return (own.astype(f32) + core_swap(other).astype(f32)).astype(bf16)

    grad_mid, branch_own, branch_other, small_n = [], [], [], []
    for k in chunks:
        pair = pair_sum(part_own[k], part_other[k])
        g, b, s = run_norm_two_back(k, middle[k], own_grad[k], pair, far_swap(pair), row(ln2_gain))
        grad_mid.append(g)
        branch_own.append(b)
        branch_other.append(core_swap(b))
        small_n.append(s)

    gproj, small_a, one_own, one_other = [], [], [], []
    for k in chunks:
        g, po, pt, s = run_attention_backward(k, items, heads, meta, branch_own[k], branch_other[k], w_out, proj[k], w_t)
        gproj.append(g)
        one_own.append(po)
        one_other.append(pt)
        small_a.append(s)
    grad_attn_part = run_attention_grads(items, heads, meta, gproj, normed_one, ctx, branch_own, branch_other)

    grad_own, small_o = [], []
    for k in chunks:
        pair = pair_sum(one_own[k], one_other[k])
        g, s = run_norm_one_back(k, meta, tokens, grad_mid[k], pair, far_swap(pair), row(ln1_gain))
        grad_own.append(g)
        small_o.append(s)
    grad_tokens = run_assemble(items, meta, grad_own, [core_swap(g) for g in grad_own], "grad_tokens")

    out_own = []
    for k in chunks:
        pair = pair_sum(down_own[k], down_other[k])
        out_own.append(run_output_rows(k, items, meta, middle[k], pair, far_swap(pair), down_bias3))
    output = run_assemble(items, meta, out_own, [core_swap(o) for o in out_own], "output")

    grad_down = sum_over_items(grad_down_part, dp)
    grad_up = sum_over_items(grad_up_part, dp)
    grad_attn = sum_over_items(grad_attn_part, dp)

    norms = jnp.concatenate([sum(small_n)[:3], sum(small_o)[:2], jnp.zeros((3, d), f32)])
    norms = norms + core_swap(norms)
    projected = jnp.pad(sum(small_a)[:1], ((0, 0), (0, d - 3 * width)))
    small = jnp.concatenate([norms, sum(small_e)[:4], projected, jnp.zeros((3, d), f32)])
    small = sum_over(small, "dp", dp)

    grad_qkv = grad_attn[: 3 * width].reshape(3, width, d).transpose(2, 0, 1)
    grad_out = grad_attn[3 * width :]
    grad_qv_bias = jnp.stack([small[12, :width], small[12, 2 * width : 3 * width]])
    return (
        output,
        grad_tokens,
        small[3],
        small[4],
        grad_qkv,
        grad_qv_bias,
        grad_out,
        small[2],
        small[0],
        small[1],
        grad_up,
        small[8:10],
        grad_down,
        small[10:12],
        totals.astype(jnp.int32),
    )


def solution(mesh):
    in_specs = (
        P("dp", None),
        P("dp"),
        P("dp"),
        P("dp", None),
        P(),
        P(),
        P(None, None, "tensor"),
        P(None, "tensor"),
        P("tensor", None),
        P(),
        P(),
        P(),
        P(None, None, "tensor"),
        P(None, "tensor"),
        P(None, "tensor", None),
        P(),
    )
    out_specs = (
        P("dp", None),
        P("dp", None),
        P(),
        P(),
        P(None, None, "tensor"),
        P(None, "tensor"),
        P("tensor", None),
        P(),
        P(),
        P(),
        P(None, None, "tensor"),
        P(None, "tensor"),
        P(None, "tensor", None),
        P(),
        P(),
    )
    return jax.shard_map(
        functools.partial(local, mesh.shape["dp"], mesh.shape["tensor"]),
        mesh=mesh,
        in_specs=in_specs,
        out_specs=out_specs,
        check_vma=False,
    )
```

time: 1190 us -> 484 us (0.41)
  blocking collectives: 636 us -> 0 us
  local copies, waits for them, and re-layouts: 239 us -> 30.9 us
  waiting for transfers between devices: 152 us -> 328 us
  matrix products: 76.2 us -> 0 us
  Pallas kernels: 0 us -> 55.1 us
  other arithmetic: 41.9 us -> 18.2 us
  starting transfers between devices: 6.9 us -> 24.9 us
    unnamed x5 -> x0, blocking collectives: 571 us -> none
    reduce_scatter x0 -> x3, waiting for transfers between devices: none -> 192 us  [sum_over_items(): share = lax.psum_scatter(flat, 'dp', scatter_dimension=0, tiled=True)]
    unnamed x10 -> x6, waiting for transfers between devices: 152 us -> 0.1 us
    unnamed x125 -> x90, local copies, waits for them, and re-layouts: 145 us -> 21.9 us
    all_gather x4 -> x3, waiting for transfers between devices: 0.02 us -> 88.2 us  [sum_over_items(): lax.all_gather(share, 'dp', axis=0, tiled=True).reshape(piece.shape)]
    dot_general x22 -> x0, matrix products: 72.2 us -> none  [the longest x1 12.1 us: local(): jnp.einsum('ie,idf->edf', item_rows, grad_up_items, precision=highest)]
    psum x2 -> x0, blocking collectives: 64.5 us -> none  [the longest x1 42.2 us: local(): lax.psum((grad_ln1_gain, grad_ln1_bias, grad_out_bias, grad_ln2_gain, gra...]
    pallas_call x0 -> x17, Pallas kernels: none -> 55.1 us  [call(): pl.pallas_call(kernel, out_shape=list(outs), in_specs=list(specs), out_sp...]
  transfers between devices with their start and end apart: 9 -> 40, of which waited for: 1 -> 16; matrix products, arithmetic and copies ran while one was open for 28% -> 5% of each run, Pallas kernels for 0% -> 10%
where the time goes in v1:
time: 484 us; the launch traced here: 475 us
  waiting for transfers between devices  328 us (68%)
  Pallas kernels  55.1 us (11%)
  local copies, waits for them, and re-layouts  30.9 us (6%)
  starting transfers between devices  24.9 us (5%)
  other arithmetic  18.2 us (4%)
  between operations  17.7 us (4%)
    reduce_scatter x3, waiting for transfers between devices, sum_over_items(): share = lax.psum_scatter(flat, 'dp', scatter_dimension=0, tiled=True)  192 us
    all_gather x3, waiting for transfers between devices, sum_over_items(): lax.all_gather(share, 'dp', axis=0, tiled=True).reshape(piece.shape)  88.2 us
    pallas_call x17, Pallas kernels, call(): pl.pallas_call(kernel, out_shape=list(outs), in_specs=list(specs), out_sp...  55.1 us
    ppermute x34, waiting for transfers between devices, swap(): return lax.ppermute(value, axis, [(i, i ^ bit) for i in range(size)])  47.5 us
    ppermute x34, starting transfers between devices, swap(): return lax.ppermute(value, axis, [(i, i ^ bit) for i in range(size)])  24.4 us
    unnamed x90, local copies, waits for them, and re-layouts  21.9 us
  transfers between devices with their start and end apart: 40, of which 16 were waited for; matrix products, arithmetic and copies ran while one was open for 5% of the time, Pallas kernels for 10%

profile of v1, /device:TPU:0, one launch (start us, length us, event | category | flops | bytes accessed | tf_op | source)
XLA Modules:
  0.0 474.9 jit_solution(18375092152161495579)
XLA Ops:
  7.2 3.0 collective-permute-start.7
  16.9 3.5 attention_forward_0.1
  27.6 3.5 attention_forward_1.1
  37.9 2.6 collective-permute-start.2
  48.8 8.5 %experts_0.1 = (f32[240,768]{1,0:T(8,128)S(1)}, f32[240,768]{1,0:T(8,128)S(1)}, bf16[2,240,768]{2,1,0:T(8,128)(2,1)S(1)}, bf16[2,240,768]{2,1,0:T(8,128)(2,1)}, ...) custom-call(s32[16]{0:T(128)S(1)} %pad_add_fusion.meta, ...), custom_call_target="tpu_custom_call" | custom-call | flops 2831155200 | bytes 15486032 | tf_op jit(solution)/shard_map/experts_0/pallas_call | solution.py:67
  60.9 8.4 %experts_1.1 = (f32[240,768]{1,0:T(8,128)S(1)}, f32[240,768]{1,0:T(8,128)S(1)}, bf16[2,240,768]{2,1,0:T(8,128)(2,1)S(1)}, bf16[2,240,768]{2,1,0:T(8,128)(2,1)}, ...) custom-call(s32[16]{0:T(128)S(1)} %pad_add_fusion.meta, ...), custom_call_target="tpu_custom_call" | custom-call | flops 2831155200 | bytes 15486032 | tf_op jit(solution)/shard_map/experts_1/pallas_call | solution.py:67
  72.5 8.8 %collective-permute-done.19.far = bf16[240,768]{1,0:T(8,128)(2,1)S(1)} collective-permute-done((bf16[240,768]{1,0:T(8,128)(2,1)S(1)}, bf16[240,768]{1,0:T(8,128)(2,1)S(1)}, u32[]{:S(2)}, u32[]{:S(2)}) %collective-permute-start.19) | collective-permute-done | bytes 368672 | tf_op jit(solution)/shard_map/ppermute | solution.py:449
  82.9 5.5 %collective-permute-done.24.far = bf16[240,768]{1,0:T(8,128)(2,1)S(1)} collective-permute-done((bf16[240,768]{1,0:T(8,128)(2,1)S(1)}, bf16[240,768]{1,0:T(8,128)(2,1)S(1)}, u32[]{:S(2)}, u32[]{:S(2)}) %collective-permute-start.24) | collective-permute-done | bytes 368672 | tf_op jit(solution)/shard_map/ppermute | solution.py:449
  90.0 5.1 %attention_backward_0.1 = (bf16[2,240,576]{2,1,0:T(8,128)(2,1)S(1)}, bf16[240,768]{1,0:T(8,128)(2,1)S(1)}, bf16[240,768]{1,0:T(8,128)(2,1)S(1)}, f32[8,576]{1,0:T(8,128)S(1)}) custom-call(s32[16]{0:T(128)S(1)} %pad_add_fusion.meta, bf16[240,768]{1,0:T(8,128)(2,1)S(1)} %get-tuple-element.73.own.refs_6_, ...), custom_call_target="tpu_custom_call" | custom-call | flops 787415040 | bytes 3778624 | tf_op jit(solution)/shard_map/attention_backward_0/pallas_call | solution.py:67
  96.6 5.4 %attention_backward_1.1 = (bf16[2,240,576]{2,1,0:T(8,128)(2,1)S(1)}, bf16[240,768]{1,0:T(8,128)(2,1)S(1)}, bf16[240,768]{1,0:T(8,128)(2,1)S(1)}, f32[8,576]{1,0:T(8,128)S(1)}) custom-call(s32[16]{0:T(128)S(1)} %pad_add_fusion.meta, bf16[240,768]{1,0:T(8,128)(2,1)S(1)} %get-tuple-element.82.own.refs_7_, ...), custom_call_target="tpu_custom_call" | custom-call | flops 787415040 | bytes 3778624 | tf_op jit(solution)/shard_map/attention_backward_1/pallas_call | solution.py:67
  103.5 3.0 attention_grads.1
  110.0 4.1 up_grads.1
  118.5 4.1 down_grads.1
  122.7 48.4 %reduce-scatter.4.cloned.1.call-done = bf16[96,768]{1,0:T(8,128)(2,1)} async-done(((bf16[768,768]{1,0:T(8,128)(2,1)}), bf16[96,768]{1,0:T(8,128)(2,1)}) %reduce-scatter.4.cloned.1.call-update) | async-done | bytes 147472 | tf_op jit(solution)/shard_map/reduce_scatter | solution.py:462
  171.2 72.0 %reduce-scatter.6.cloned.1.call-done = bf16[192,768]{1,0:T(8,128)(2,1)} async-done(((bf16[1536,768]{1,0:T(8,128)(2,1)}), bf16[192,768]{1,0:T(8,128)(2,1)}) %reduce-scatter.6.cloned.1.call-update) | async-done | bytes 294928 | tf_op jit(solution)/shard_map/reduce_scatter | solution.py:462
  243.6 71.9 %reduce-scatter.8.cloned.1.call-done = bf16[192,768]{1,0:T(8,128)(2,1)} async-done(((bf16[1536,768]{1,0:T(8,128)(2,1)}), bf16[192,768]{1,0:T(8,128)(2,1)}) %reduce-scatter.8.cloned.1.call-update) | async-done | bytes 294928 | tf_op jit(solution)/shard_map/reduce_scatter | solution.py:462
  325.3 12.7 %collective-permute-done.22.far = bf16[240,768]{1,0:T(8,128)(2,1)S(1)} collective-permute-done((bf16[240,768]{1,0:T(8,128)(2,1)S(1)}, bf16[240,768]{1,0:T(8,128)(2,1)S(1)}, u32[]{:S(2)}, u32[]{:S(2)}) %collective-permute-start.22) | collective-permute-done | bytes 368672 | tf_op jit(solution)/shard_map/ppermute | solution.py:449
  339.2 6.6 %collective-permute-done.27.far = bf16[240,768]{1,0:T(8,128)(2,1)S(1)} collective-permute-done((bf16[240,768]{1,0:T(8,128)(2,1)S(1)}, bf16[240,768]{1,0:T(8,128)(2,1)S(1)}, u32[]{:S(2)}, u32[]{:S(2)}) %collective-permute-start.27) | collective-permute-done | bytes 368672 | tf_op jit(solution)/shard_map/ppermute | solution.py:449
  350.1 2.9 collective-permute-done.15.far
  354.7 3.5 collective-permute-done.32
  371.0 39.7 %all-gather.6.cloned.1.call-done = bf16[1536,768]{1,0:T(8,128)(2,1)} async-done(((bf16[192,768]{1,0:T(8,128)(2,1)}), bf16[1536,768]{1,0:T(8,128)(2,1)}) %all-gather.6.cloned.1.call-update) | async-done | bytes 2359312 | tf_op jit(solution)/shard_map/all_gather | solution.py:463
  410.7 4.2 convert.2
  415.0 48.5 %all-gather.8.cloned.1.call-done = bf16[1536,768]{1,0:T(8,128)(2,1)} async-done(((bf16[192,768]{1,0:T(8,128)(2,1)}), bf16[1536,768]{1,0:T(8,128)(2,1)}) %all-gather.8.cloned.1.call-update) | async-done | bytes 2359312 | tf_op jit(solution)/shard_map/all_gather | solution.py:463
  463.4 4.2 convert.3
  (219 shorter events, 77.1 us)
Async XLA Ops:
  7.2 163.9 %reduce-scatter.4.cloned.1.call-start = ((), (), s32[]{:S(2)}) async-start(), calls=%async_computation.3 | async-start | bytes 1327104 | tf_op jit(solution)/shard_map/reduce_scatter | solution.py:462
  7.2 37.2 %collective-permute-start.7 = (bf16[192,768]{1,0:T(8,128)(2,1)}, bf16[192,768]{1,0:T(8,128)(2,1)S(1)}, u32[]{:S(2)}, u32[]{:S(2)}) collective-permute-start(bf16[192,768]{1,0:T(8,128)(2,1)} %w_out.3), channel_id=1, source_target_pairs={{0,2},{1,3},{2,0},{3,1},{4,6},{5,7},{6,4},{7,5},{8,10},{9,11},{10,... | collective-permute-start | bytes 884744 | tf_op jit(solution)/shard_map/ppermute | solution.py:449
  10.3 38.5 %collective-permute-start.6 = (bf16[192,768]{1,0:T(8,128)(2,1)}, bf16[192,768]{1,0:T(8,128)(2,1)}, u32[]{:S(2)}, u32[]{:S(2)}) collective-permute-start(bf16[192,768]{1,0:T(8,128)(2,1)} %w_out.3), channel_id=1, source_target_pairs={{0,1},{1,0},{2,3},{3,2},{4,5},{5,4},{6,7},{7,6},{8,9},{9,8},{10,11... | collective-permute-start | bytes 884744 | tf_op jit(solution)/shard_map/ppermute | solution.py:449
  22.1 24.2 %collective-permute-start.4 = (bf16[240,384]{1,0:T(8,128)(2,1)S(1)}, bf16[240,384]{1,0:T(8,128)(2,1)}, u32[]{:S(2)}, u32[]{:S(2)}) collective-permute-start(bf16[240,384]{1,0:T(8,128)(2,1)S(1)} %get-tuple-element.61.c0.refs_4_), channel_id=1, source_target_pairs={{0,2},{1,3},{2,0},{3,1},{4,6},{5,7},{6,4},{7,5},{8,10},{9,11},{10,... | collective-permute-start | bytes 552968 | tf_op jit(solution)/shard_map/ppermute | solution.py:449
  22.2 26.1 %collective-permute-start.3 = (bf16[240,384]{1,0:T(8,128)(2,1)S(1)}, bf16[240,384]{1,0:T(8,128)(2,1)}, u32[]{:S(2)}, u32[]{:S(2)}) collective-permute-start(bf16[240,384]{1,0:T(8,128)(2,1)S(1)} %get-tuple-element.61.c0.refs_4_), channel_id=1, source_target_pairs={{0,1},{1,0},{2,3},{3,2},{4,5},{5,4},{6,7},{7,6},{8,9},{9,8},{10,11... | collective-permute-start | bytes 552968 | tf_op jit(solution)/shard_map/ppermute | solution.py:449
  25.9 7.0 %collective-permute-start = (f32[2]{0:T(128)S(1)}, f32[2]{0:T(128)S(1)}, u32[]{:S(2)}, u32[]{:S(2)}) collective-permute-start(f32[2]{0:T(128)S(1)} %add_convert_fusion.6), channel_id=1, source_target_pairs={{0,4},{4,0},{8,12},{12,8},{16,20},{20,16},{24,28},{28,24},{1,5},{5... | collective-permute-start | bytes 32 | tf_op jit(solution)/shard_map/ppermute | solution.py:449
  48.2 10.7 %collective-permute-start.11 = (bf16[240,384]{1,0:T(8,128)(2,1)S(1)}, bf16[240,384]{1,0:T(8,128)(2,1)S(1)}, u32[]{:S(2)}, u32[]{:S(2)}) collective-permute-start(bf16[240,384]{1,0:T(8,128)(2,1)S(1)} %get-tuple-element.65.c0.refs_5_), channel_id=1, source_target_pairs={{0,1},{1,0},{2,3},{3,2},{4,5},{5,4},{6,7},{7,6},{8,9},{9,8},{10,11... | collective-permute-start | bytes 552968 | tf_op jit(solution)/shard_map/ppermute | solution.py:449
  48.3 10.6 %collective-permute-start.13 = (bf16[240,384]{1,0:T(8,128)(2,1)}, bf16[240,384]{1,0:T(8,128)(2,1)S(1)}, u32[]{:S(2)}, u32[]{:S(2)}) collective-permute-start(bf16[240,384]{1,0:T(8,128)(2,1)} %collective-permute-done.12.c2), channel_id=1, source_target_pairs={{0,1},{1,0},{2,3},{3,2},{4,5},{5,4},{6,7},{7,6},{8,9},{9,8},{10,11... | collective-permute-start | bytes 552968 | tf_op jit(solution)/shard_map/ppermute | solution.py:449
  58.8 10.9 %collective-permute-start.18 = (bf16[240,768]{1,0:T(8,128)(2,1)S(1)}, bf16[240,768]{1,0:T(8,128)(2,1)S(1)}, u32[]{:S(2)}, u32[]{:S(2)}) collective-permute-start(bf16[240,768]{1,0:T(8,128)(2,1)S(1)} %get-tuple-element.71), channel_id=1, source_target_pairs={{0,1},{1,0},{2,3},{3,2},{4,5},{5,4},{6,7},{7,6},{8,9},{9,8},{10,11... | collective-permute-start | bytes 1105928 | tf_op jit(solution)/shard_map/ppermute | solution.py:449
  69.8 11.5 %collective-permute-start.19 = (bf16[240,768]{1,0:T(8,128)(2,1)S(1)}, bf16[240,768]{1,0:T(8,128)(2,1)S(1)}, u32[]{:S(2)}, u32[]{:S(2)}) collective-permute-start(bf16[240,768]{1,0:T(8,128)(2,1)S(1)} %add_convert_fusion.3.pair), channel_id=1, source_target_pairs={{0,2},{1,3},{2,0},{3,1},{4,6},{5,7},{6,4},{7,5},{8,10},{9,11},{10,... | collective-permute-start | bytes 1105928 | tf_op jit(solution)/shard_map/ppermute | solution.py:449
  71.3 17.1 %collective-permute-start.24 = (bf16[240,768]{1,0:T(8,128)(2,1)S(1)}, bf16[240,768]{1,0:T(8,128)(2,1)S(1)}, u32[]{:S(2)}, u32[]{:S(2)}) collective-permute-start(bf16[240,768]{1,0:T(8,128)(2,1)S(1)} %add_convert_fusion.1.pair), channel_id=1, source_target_pairs={{0,2},{1,3},{2,0},{3,1},{4,6},{5,7},{6,4},{7,5},{8,10},{9,11},{10,... | collective-permute-start | bytes 1105928 | tf_op jit(solution)/shard_map/ppermute | solution.py:449
  82.9 7.1 %collective-permute-start.20 = (bf16[240,768]{1,0:T(8,128)(2,1)S(1)}, bf16[240,768]{1,0:T(8,128)(2,1)S(1)}, u32[]{:S(2)}, u32[]{:S(2)}) collective-permute-start(bf16[240,768]{1,0:T(8,128)(2,1)S(1)} %get-tuple-element.73.own.refs_6_), channel_id=1, source_target_pairs={{0,1},{1,0},{2,3},{3,2},{4,5},{5,4},{6,7},{7,6},{8,9},{9,8},{10,11... | collective-permute-start | bytes 1105928 | tf_op jit(solution)/shard_map/ppermute | solution.py:449
  90.0 6.7 %collective-permute-start.25 = (bf16[240,768]{1,0:T(8,128)(2,1)S(1)}, bf16[240,768]{1,0:T(8,128)(2,1)S(1)}, u32[]{:S(2)}, u32[]{:S(2)}) collective-permute-start(bf16[240,768]{1,0:T(8,128)(2,1)S(1)} %get-tuple-element.82.own.refs_7_), channel_id=1, source_target_pairs={{0,1},{1,0},{2,3},{3,2},{4,5},{5,4},{6,7},{7,6},{8,9},{9,8},{10,11... | collective-permute-start | bytes 1105928 | tf_op jit(solution)/shard_map/ppermute | solution.py:449
  106.6 136.7 %reduce-scatter.6.cloned.1.call-start = ((), (), s32[]{:S(2)}) async-start(), calls=%async_computation.5 | async-start | bytes 2654208 | tf_op jit(solution)/shard_map/reduce_scatter | solution.py:462
  114.1 201.4 %reduce-scatter.8.cloned.1.call-start = ((), (), s32[]{:S(2)}) async-start(), calls=%async_computation.7 | async-start | bytes 2654208 | tf_op jit(solution)/shard_map/reduce_scatter | solution.py:462
  122.6 245.1 %all-gather.4.cloned.1.call-start = ((), (), s32[]{:S(2)}) async-start(), calls=%async_computation.4 | async-start | bytes 1327104 | tf_op jit(solution)/shard_map/all_gather | solution.py:463
  171.1 239.6 %all-gather.6.cloned.1.call-start = ((), (), s32[]{:S(2)}) async-start(), calls=%async_computation.6 | async-start | bytes 2654208 | tf_op jit(solution)/shard_map/all_gather | solution.py:463
  243.3 220.2 %all-gather.8.cloned.1.call-start = ((), (), s32[]{:S(2)}) async-start(), calls=%async_computation.8 | async-start | bytes 2654208 | tf_op jit(solution)/shard_map/all_gather | solution.py:463
  315.6 8.9 %collective-permute-start.14 = (bf16[240,768]{1,0:T(8,128)(2,1)}, bf16[240,768]{1,0:T(8,128)(2,1)S(1)}, u32[]{:S(2)}, u32[]{:S(2)}) collective-permute-start(bf16[240,768]{1,0:T(8,128)(2,1)} %copy-done.25), channel_id=1, source_target_pairs={{0,1},{1,0},{2,3},{3,2},{4,5},{5,4},{6,7},{7,6},{8,9},{9,8},{10,11... | collective-permute-start | bytes 1105928 | tf_op jit(solution)/shard_map/ppermute | solution.py:449
  318.6 30.8 %collective-permute-start.10 = (bf16[240,768]{1,0:T(8,128)(2,1)S(1)}, bf16[240,768]{1,0:T(8,128)(2,1)S(1)}, u32[]{:S(2)}, u32[]{:S(2)}) collective-permute-start(bf16[240,768]{1,0:T(8,128)(2,1)S(1)} %add_convert_fusion.5.pair), channel_id=1, source_target_pairs={{0,2},{1,3},{2,0},{3,1},{4,6},{5,7},{6,4},{7,5},{8,10},{9,11},{10,... | collective-permute-start | bytes 1105928 | tf_op jit(solution)/shard_map/ppermute | solution.py:449
  321.2 16.8 %collective-permute-start.22 = (bf16[240,768]{1,0:T(8,128)(2,1)S(1)}, bf16[240,768]{1,0:T(8,128)(2,1)S(1)}, u32[]{:S(2)}, u32[]{:S(2)}) collective-permute-start(bf16[240,768]{1,0:T(8,128)(2,1)S(1)} %add_convert_fusion.2.pair), channel_id=1, source_target_pairs={{0,2},{1,3},{2,0},{3,1},{4,6},{5,7},{6,4},{7,5},{8,10},{9,11},{10,... | collective-permute-start | bytes 1105928 | tf_op jit(solution)/shard_map/ppermute | solution.py:449
  323.0 22.9 %collective-permute-start.27 = (bf16[240,768]{1,0:T(8,128)(2,1)S(1)}, bf16[240,768]{1,0:T(8,128)(2,1)S(1)}, u32[]{:S(2)}, u32[]{:S(2)}) collective-permute-start(bf16[240,768]{1,0:T(8,128)(2,1)S(1)} %add_convert_fusion.pair), channel_id=1, source_target_pairs={{0,2},{1,3},{2,0},{3,1},{4,6},{5,7},{6,4},{7,5},{8,10},{9,11},{10,... | collective-permute-start | bytes 1105928 | tf_op jit(solution)/shard_map/ppermute | solution.py:449
  324.6 28.3 %collective-permute-start.15 = (bf16[240,768]{1,0:T(8,128)(2,1)S(1)}, bf16[240,768]{1,0:T(8,128)(2,1)S(1)}, u32[]{:S(2)}, u32[]{:S(2)}) collective-permute-start(bf16[240,768]{1,0:T(8,128)(2,1)S(1)} %add_convert_fusion.4.pair), channel_id=1, source_target_pairs={{0,2},{1,3},{2,0},{3,1},{4,6},{5,7},{6,4},{7,5},{8,10},{9,11},{10,... | collective-permute-start | bytes 1105928 | tf_op jit(solution)/shard_map/ppermute | solution.py:449
  350.0 9.5 %collective-permute-start.16 = (bf16[240,768]{1,0:T(8,128)(2,1)S(1)}, bf16[240,768]{1,0:T(8,128)(2,1)S(1)}, u32[]{:S(2)}, u32[]{:S(2)}) collective-permute-start(bf16[240,768]{1,0:T(8,128)(2,1)S(1)} %output_rows_0.1.refs_0_), channel_id=1, source_target_pairs={{0,1},{1,0},{2,3},{3,2},{4,5},{5,4},{6,7},{7,6},{8,9},{9,8},{10,11... | collective-permute-start | bytes 1105928 | tf_op jit(solution)/shard_map/ppermute | solution.py:449
  (61 other events, 435.1 us)
Sparse Core Ops, SparseCore 0:
  106.7 64.3 reduce-scatter.3
  175.2 68.0 reduce-scatter.5
  247.3 68.1 reduce-scatter.7
  317.5 40.2 all-gather.3
  359.9 50.8 all-gather.5
  412.8 50.5 all-gather.7

commit v2 on v1

v2 whole, which is shorter than its diff:
```python
import functools

import jax
import jax.numpy as jnp
from jax import lax
from jax.experimental import pallas as pl
from jax.experimental.pallas import tpu as pltpu
from jax.sharding import PartitionSpec as P

HEAD = 64
PATCHES = 197
CAP = 40
SEQ = PATCHES + CAP
PAD = 240
ATT = 256
STAGE = 2 * SEQ + 32

epsilon = 1e-05
f32 = jnp.float32
bf16 = jnp.bfloat16

NT = (((1,), (1,)), ((), ()))
NN = (((1,), (0,)), ((), ()))
TN = (((0,), (0,)), ((), ()))

VMEM = pltpu.VMEM
SMEM = pltpu.SMEM


def dot(a, b, dims=NN):
    return lax.dot_general(a, b, dims, preferred_element_type=f32)


def iota(shape, dim):
    return lax.broadcasted_iota(jnp.int32, shape, dim)


def unit_rows(x):
    mean = jnp.mean(x, -1, keepdims=True)
    centered = x - mean
    scale = lax.rsqrt(jnp.mean(centered * centered, -1, keepdims=True) + epsilon)
    return centered * scale, scale


def norm_back(grad, unit, scale, gain):
    t = grad * gain
    return scale * (
        t - jnp.mean(t, -1, keepdims=True) - unit * jnp.mean(t * unit, -1, keepdims=True)
    )


def line(ref):
    return ref[...].reshape(1, -1)


def vspec():
    return pl.BlockSpec(memory_space=VMEM)


def sspec():
    return pl.BlockSpec(memory_space=SMEM)


def aspec():
    return pl.BlockSpec(memory_space=pl.ANY)


class Order:
    def __init__(self):
        self.last = None

    def __call__(self, kernel, ins, specs, outs, scratch=(), limit=16, flops=0, name=None):
        size = sum(a.size * a.dtype.itemsize for a in ins)
        size += sum(o.size * o.dtype.itemsize for o in outs)
        taken = len(ins)
        behind = () if self.last is None or any(a is self.last for a in ins) else (self.last,)

        def body(*refs):
            kernel(*refs[:taken], *refs[taken + len(behind) :])

        results = pl.pallas_call(
            body,
            out_shape=list(outs),
            in_specs=list(specs) + [aspec() for _ in behind],
            out_specs=[vspec() for _ in outs],
            scratch_shapes=list(scratch),
            compiler_params=pltpu.CompilerParams(vmem_limit_bytes=limit * 1024 * 1024),
            cost_estimate=pl.CostEstimate(
                flops=int(flops), bytes_accessed=int(size), transcendentals=0
            ),
            name=name,
        )(*ins, *behind)
        self.last = results[0]
        return results


def arr(shape, dtype):
    return jax.ShapeDtypeStruct(shape, dtype)


def position():
    return lax.axis_index("tensor")


def is_first():
    return lax.rem(position(), 2) == 0


def places():
    place = lax.axis_index("dp")
    low = lax.rem(place, 2)
    high = lax.rem(lax.div(place, 2), 2)
    first = is_first()
    return jnp.where(first, low, high), jnp.where(first, high, low)


def live_rows(mask, item):
    count = PATCHES
    for slot in range(CAP):
        count = count + mask[item * SEQ + PATCHES + slot]
    return count


def expert_of(kind, item):
    return kind[item * SEQ]


def stage_rows(ref, buf, chunk):
    low = 2 * chunk * SEQ
    high = low + 2 * SEQ
    base = low // 16 * 16
    top = min(ref.shape[0], -(-high // 16) * 16)
    buf[0 : top - base] = ref[...][base:top].astype(f32)
    return [low - base, low - base + SEQ]


def item_rows(buf, offset, count, live=SEQ):
    rows = buf[pl.ds(offset, count), :]
    return jnp.where(iota(rows.shape, 0) < live, rows, 0.0)


def count_rows(items, mask, kind, out):
    total = 0
    second = 0
    for i in range(items):
        n = live_rows(mask, i)
        total = total + n
        second = second + n * expert_of(kind, i)
    row = iota(out.shape, 0)
    out[...] = jnp.where(row == 0, total - second, second).astype(f32)


def run_count_rows(call, items, mask, kind):
    return call(
        functools.partial(count_rows, items), (mask, kind), [sspec()] * 2, [arr((8, 128), f32)], limit=4, name="count"
    )[0]


def row_weight(counts):
    both = counts[0:1, 0:1] + counts[1:2, 0:1]
    return both / (2.0 * counts[0:1, 0:1]), both / (2.0 * counts[1:2, 0:1])


def attention_forward(chunk, heads, mask, tokens, w_t, qv_bias, gain, bias, ctx, proj, normed, buf):
    width = heads * HEAD
    offsets = stage_rows(tokens, buf, chunk)
    b_three = jnp.concatenate([qv_bias[0:1, :], jnp.zeros((1, width), f32), qv_bias[1:2, :]], axis=1)
    for j in range(2):
        live = live_rows(mask, 2 * chunk + j)
        x = item_rows(buf, offsets[j], ATT)
        unit, _ = unit_rows(x)
        n_row = (unit * line(gain) + line(bias)).astype(bf16)
        normed[j] = n_row[:PAD]
        p_row = (dot(n_row, w_t[...], NT) + b_three).astype(bf16)
        proj[j] = p_row[:PAD]
        key_live = iota((ATT, ATT), 1) < live
        for h in range(heads):
            q = p_row[:, h * HEAD : (h + 1) * HEAD]
            k = p_row[:, width + h * HEAD : width + (h + 1) * HEAD]
            v = p_row[:, 2 * width + h * HEAD : 2 * width + (h + 1) * HEAD]
            s = jnp.where(key_live, dot(q, k, NT) * 0.125, -1e30)
            e = jnp.exp(s - jnp.max(s, -1, keepdims=True))
            att = (e * (1.0 / jnp.sum(e, -1, keepdims=True))).astype(bf16)
            c = dot(att, v).astype(bf16)
            at = j * width + h * HEAD
            ctx[:, at : at + HEAD] = c[:PAD]


def run_attention_forward(call, chunk, heads, mask, tokens, w_t, qv_bias, gain, bias):
    width = heads * HEAD
    d = tokens.shape[1]
    return call(
        functools.partial(attention_forward, chunk, heads),
        (mask, tokens, w_t, qv_bias, gain, bias),
        [sspec()] + [vspec()] * 5,
        [arr((PAD, 2 * width), bf16), arr((2, PAD, 3 * width), bf16), arr((2, PAD, d), bf16)],
        [VMEM((STAGE, d), f32)],
        flops=2 * 2 * ATT * (d * 3 * width + 4 * ATT * width),
        name="attention_forward_%d" % chunk,
    )


def gelu_parts(h):
    cdf = 0.5 * (1.0 + lax.erf(h * 0.7071067811865476))
    density = jnp.exp(-0.5 * h * h) * 0.3989422804014327
    return h * cdf, cdf + h * density


def experts(
    chunk, heads, mask, kind, tokens, cot, c0, c1, c2, c3, o0, o1, o2, o3, out_bias, gain, bias,
    up_bias, w_up, w_down,
    middle, masked, normed, active, ghid, down_own, down_other, part_own, part_other, small,
    buf, cbuf, ctx, w_out,
):
    width = heads * HEAD
    d = tokens.shape[1]
    t = position()
    core = lax.rem(t, 2)
    first = core == 0
    slots = (t, t + 1 - 2 * core, lax.rem(t + 2, 4), lax.rem(t + 3 - 2 * core, 4))
    for slot, c, o in zip(slots, (c0, c1, c2, c3), (o0, o1, o2, o3)):
        ctx[slot] = c[...]
        w_out[slot] = o[...]
    offsets = stage_rows(tokens, buf, chunk)
    cot_offsets = stage_rows(cot, cbuf, chunk)
    mids, cots, n_rows = [], [], []
    for j in range(2):
        x = item_rows(buf, offsets[j], PAD)
        total = jnp.zeros((PAD, d), f32)
        for s in range(4):
            total = total + dot(ctx[s][:, j * width : (j + 1) * width], w_out[s])
        mid = x + total + line(out_bias)
        mids.append(mid)
        unit, _ = unit_rows(mid)
        n_row = (unit * line(gain) + line(bias)).astype(bf16)
        normed[j] = n_row
        n_rows.append(n_row)
        c_row = item_rows(cbuf, cot_offsets[j], PAD, live_rows(mask, 2 * chunk + j)).astype(bf16)
        masked[j] = c_row
        cots.append(c_row)
    middle[...] = jnp.where(first, mids[0], mids[1])
    small[...] = jnp.zeros_like(small)
    parts, downs = [], []
    for j in range(2):
        e = expert_of(kind, 2 * chunk + j)
        wu = w_up[e]
        wd = w_down[e]
        h = dot(n_rows[j], wu) + up_bias[pl.ds(e, 1), :]
        value, slope = gelu_parts(h)
        act = value.astype(bf16)
        active[j] = act
        gh = (dot(cots[j], wd, NT) * slope).astype(bf16)
        ghid[j] = gh
        parts.append(dot(gh, wu, NT))
        downs.append(dot(act, wd))
        small[pl.ds(e, 1), :] += jnp.sum(gh.astype(f32), 0, keepdims=True)
        small[pl.ds(e + 2, 1), :] += jnp.sum(cots[j].astype(f32), 0, keepdims=True)
    part_own[...] = jnp.where(first, parts[0], parts[1]).astype(bf16)
    part_other[...] = jnp.where(first, parts[1], parts[0]).astype(bf16)
    down_own[...] = jnp.where(first, downs[0], downs[1]).astype(bf16)
    down_other[...] = jnp.where(first, downs[1], downs[0]).astype(bf16)


def run_experts(
    call, chunk, heads, mask, kind, tokens, cot, ctxs, outs, out_bias, gain, bias, up_bias, w_up, w_down
):
    width = heads * HEAD
    d = tokens.shape[1]
    ff = w_up.shape[2]
    row = arr((PAD, d), bf16)
    return call(
        functools.partial(experts, chunk, heads),
        (mask, kind, tokens, cot, *ctxs, *outs, out_bias, gain, bias, up_bias, w_up, w_down),
        [sspec()] * 2 + [vspec()] * 16,
        [
            arr((PAD, d), f32),
            arr((2, PAD, d), bf16),
            arr((2, PAD, d), bf16),
            arr((2, PAD, ff), bf16),
            arr((2, PAD, ff), bf16),
            row,
            row,
            row,
            row,
            arr((8, d), f32),
        ],
        [
            VMEM((STAGE, d), f32),
            VMEM((STAGE, d), f32),
            VMEM((4, PAD, 2 * width), bf16),
            VMEM((4, width, d), bf16),
        ],
        flops=2 * 2 * PAD * d * (4 * width + 4 * ff),
        limit=24,
        name="experts_%d" % chunk,
    )


def expert_grads(items, kind, counts, *refs):
    chunks = items // 2
    lefts, rights = refs[:chunks], refs[chunks : 2 * chunks]
    send, keep, total = refs[2 * chunks :]
    for i in range(items):
        e = expert_of(kind, i)
        term = dot(lefts[i // 2][i % 2], rights[i // 2][i % 2], TN)
        if i == 0:
            total[e] = term
            total[1 - e] = jnp.zeros_like(term)
        else:
            total[e] += term
    first, second = row_weight(counts)
    one, _ = places()
    keep[...] = (total[one] * jnp.where(one == 0, first, second)).astype(bf16)
    send[...] = (total[1 - one] * jnp.where(one == 0, second, first)).astype(bf16)


def run_expert_grads(call, items, kind, counts, lefts, rights, name):
    shape = (lefts[0].shape[2], rights[0].shape[2])
    return call(
        functools.partial(expert_grads, items),
        (kind, counts, *lefts, *rights),
        [sspec()] + [vspec()] * (1 + items),
        [arr(shape, bf16)] * 2,
        [VMEM((2, *shape), f32)],
        flops=2 * items * PAD * shape[0] * shape[1],
        name=name,
    )


def own_weight(chunk, kind, counts):
    e = jnp.where(is_first(), expert_of(kind, 2 * chunk), expert_of(kind, 2 * chunk + 1))
    first, second = row_weight(counts)
    return jnp.where(e == 0, first, second)


def norm_two_back(chunk, kind, counts, middle, masked, pair, far, gain, grad_mid, branch, small):
    weight = own_weight(chunk, kind, counts)
    unit, scale = unit_rows(middle[...])
    grad = (pair[...].astype(f32) + far[...].astype(f32)) * weight
    own_cot = jnp.where(is_first(), masked[0], masked[1]).astype(f32)
    out = own_cot * weight + norm_back(grad, unit, scale, line(gain))
    grad_mid[...] = out
    branch[...] = out.astype(bf16)
    small[...] = jnp.zeros_like(small)
    small[0:1, :] = jnp.sum(grad * unit, 0, keepdims=True)
    small[1:2, :] = jnp.sum(grad, 0, keepdims=True)
    small[2:3, :] = jnp.sum(out, 0, keepdims=True)


def run_norm_two_back(call, chunk, kind, counts, middle, masked, pair, far, gain):
    shape = middle.shape
    return call(
        functools.partial(norm_two_back, chunk),
        (kind, counts, middle, masked, pair, far, gain),
        [sspec()] + [vspec()] * 6,
        [arr(shape, f32), arr(shape, bf16), arr((8, shape[1]), f32)],
        flops=20 * middle.size,
        name="norm_two_back_%d" % chunk,
    )


def attention_backward(chunk, heads, mask, own, other, w_out, proj, w_t, gproj, part_own, part_other, small):
    width = heads * HEAD
    first = is_first()
    parts = []
    small[...] = jnp.zeros_like(small)
    for j in range(2):
        live = live_rows(mask, 2 * chunk + j)
        a, b = (own, other) if j == 0 else (other, own)
        branch = jnp.where(first, a[...], b[...])
        gctx = dot(branch, w_out[...], NT).astype(bf16)
        p_row = proj[j]
        key_live = iota((PAD, PAD), 1) < live
        gq, gk, gv = [], [], []
        for h in range(heads):
            q = p_row[:, h * HEAD : (h + 1) * HEAD]
            k = p_row[:, width + h * HEAD : width + (h + 1) * HEAD]
            v = p_row[:, 2 * width + h * HEAD : 2 * width + (h + 1) * HEAD]
            gc = gctx[:, h * HEAD : (h + 1) * HEAD]
            s = jnp.where(key_live, dot(q, k, NT) * 0.125, -1e30)
            e = jnp.exp(s - jnp.max(s, -1, keepdims=True))
            att = e * (1.0 / jnp.sum(e, -1, keepdims=True))
            ga = dot(gc, v, NT)
            gs = (att * (ga - jnp.sum(ga * att, -1, keepdims=True))).astype(bf16)
            gv.append(dot(att.astype(bf16), gc, TN))
            gq.append(dot(gs, k) * 0.125)
            gk.append(dot(gs, q, TN) * 0.125)
        gp = jnp.concatenate(gq + gk + gv, axis=1).astype(bf16)
        gproj[j] = gp
        small[0:1, :] += jnp.sum(gp.astype(f32), 0, keepdims=True)
        parts.append(dot(gp, w_t[...]))
    part_own[...] = jnp.where(first, parts[0], parts[1]).astype(bf16)
    part_other[...] = jnp.where(first, parts[1], parts[0]).astype(bf16)


def run_attention_backward(call, chunk, heads, mask, own, other, w_out, proj, w_t):
    width = heads * HEAD
    d = own.shape[1]
    return call(
        functools.partial(attention_backward, chunk, heads),
        (mask, own, other, w_out, proj, w_t),
        [sspec()] + [vspec()] * 5,
        [arr((2, PAD, 3 * width), bf16), arr((PAD, d), bf16), arr((PAD, d), bf16), arr((8, 3 * width), f32)],
        flops=2 * 2 * PAD * (d * 4 * width + 5 * PAD * width),
        name="attention_backward_%d" % chunk,
    )


def attention_grads(items, heads, *refs):
    width = heads * HEAD
    chunks = items // 2
    gproj, normed, ctx = refs[:chunks], refs[chunks : 2 * chunks], refs[2 * chunks : 3 * chunks]
    own, other = refs[3 * chunks : 4 * chunks], refs[4 * chunks : 5 * chunks]
    send, keep, both = refs[5 * chunks :]
    first = is_first()
    rows = 3 * width
    total = jnp.zeros((rows, keep.shape[1]), f32)
    total_out = jnp.zeros((width, keep.shape[1]), f32)
    for k in range(chunks):
        for j in range(2):
            total = total + dot(gproj[k][j], normed[k][j], TN)
            a, b = (own[k], other[k]) if j == 0 else (other[k], own[k])
            branch = jnp.where(first, a[...], b[...])
            total_out = total_out + dot(ctx[k][:, j * width : (j + 1) * width], branch, TN)
    half = 2 * width
    both[0] = total[:half].astype(bf16)
    both[1, 0 : rows - half] = total[half:].astype(bf16)
    both[1, rows - half :] = total_out.astype(bf16)
    one, _ = places()
    keep[...] = both[one]
    send[...] = both[1 - one]


def run_attention_grads(call, items, heads, gproj, normed, ctx, own, other):
    width = heads * HEAD
    d = own[0].shape[1]
    return call(
        functools.partial(attention_grads, items, heads),
        (*gproj, *normed, *ctx, *own, *other),
        [vspec()] * (5 * items // 2),
        [arr((2 * width, d), bf16)] * 2,
        [VMEM((2, 2 * width, d), bf16)],
        flops=2 * items * PAD * d * 4 * width,
        name="attention_grads",
    )


def norm_one_back(chunk, tokens, grad_mid, pair, far, gain, grad_own, small, buf):
    offsets = stage_rows(tokens, buf, chunk)
    x = jnp.where(is_first(), item_rows(buf, offsets[0], PAD), item_rows(buf, offsets[1], PAD))
    unit, scale = unit_rows(x)
    grad = pair[...].astype(f32) + far[...].astype(f32)
    grad_own[...] = (grad_mid[...] + norm_back(grad, unit, scale, line(gain))).astype(bf16)
    small[...] = jnp.zeros_like(small)
    small[0:1, :] = jnp.sum(grad * unit, 0, keepdims=True)
    small[1:2, :] = jnp.sum(grad, 0, keepdims=True)


def run_norm_one_back(call, chunk, tokens, grad_mid, pair, far, gain):
    shape = grad_mid.shape
    return call(
        functools.partial(norm_one_back, chunk),
        (tokens, grad_mid, pair, far, gain),
        [vspec()] * 5,
        [arr(shape, bf16), arr((8, shape[1]), f32)],
        [VMEM((STAGE, shape[1]), f32)],
        flops=20 * grad_mid.size,
        name="norm_one_back_%d" % chunk,
    )


def output_rows(chunk, kind, middle, pair, far, down_bias, out):
    e = jnp.where(is_first(), expert_of(kind, 2 * chunk), expert_of(kind, 2 * chunk + 1))
    bias = down_bias[pl.ds(e, 1), :]
    out[...] = (middle[...] + (pair[...].astype(f32) + far[...].astype(f32)) + bias).astype(bf16)


def run_output_rows(call, chunk, kind, middle, pair, far, down_bias):
    return call(
        functools.partial(output_rows, chunk),
        (kind, middle, pair, far, down_bias),
        [sspec()] + [vspec()] * 4,
        [arr(middle.shape, bf16)],
        flops=4 * middle.size,
        name="output_rows_%d" % chunk,
    )[0]


def assemble(items, *refs):
    chunks = items // 2
    own, other, out, buf = refs[:chunks], refs[chunks : 2 * chunks], refs[2 * chunks], refs[2 * chunks + 1]
    first = is_first()
    for k in range(chunks):
        for j in range(2):
            a, b = (own[k], other[k]) if j == 0 else (other[k], own[k])
            rows = jnp.where(first, a[...], b[...]).astype(f32)
            buf[pl.ds((2 * k + j) * SEQ, PAD), :] = rows
    out[...] = buf[0 : items * SEQ, :].astype(bf16)


def run_assemble(call, items, own, other, name):
    d = own[0].shape[1]
    return call(
        functools.partial(assemble, items),
        (*own, *other),
        [vspec()] * items,
        [arr((items * SEQ, d), bf16)],
        [VMEM((items * SEQ + 16, d), f32)],
        name=name,
    )[0]


def swap(value, axis, size, bit):
    return lax.ppermute(value, axis, [(i, i ^ bit) for i in range(size)])


def add_kernel(a, b, out):
    out[...] = (a[...].astype(f32) + b[...].astype(f32)).astype(out.dtype)


def run_add(call, a, b, name):
    return call(add_kernel, (a, b), [vspec()] * 2, [arr(a.shape, a.dtype)], name=name)[0]


def fold_kernel(keep, got, send_next, keep_next):
    _, two = places()
    keep_next[...] = (keep[two].astype(f32) + got[two].astype(f32)).astype(bf16)
    send_next[...] = (keep[1 - two].astype(f32) + got[1 - two].astype(f32)).astype(bf16)


def join_kernel(stage, own, other, out):
    bit = places()[stage]
    out[bit] = own[...].astype(out.dtype)
    out[1 - bit] = other[...].astype(out.dtype)


def run_join(call, stage, own, other, dtype, name):
    out = call(
        functools.partial(join_kernel, stage), (own, other), [vspec()] * 2, [arr((2, *own.shape), dtype)], name=name
    )[0]
    return out.reshape(2 * own.shape[0], *own.shape[1:])


class Sum:
    def __init__(self, call, dp, tp, name, send, keep):
        self.call, self.dp, self.tp, self.name, self.keep = call, dp, tp, name, keep
        if dp == 8:
            self.got = self.cross(send, (1, 2))
            return
        one, _ = places()
        flat = jnp.where(one == 0, jnp.concatenate([keep, send]), jnp.concatenate([send, keep]))
        share = lax.psum_scatter(flat, "dp", scatter_dimension=0, tiled=True)
        self.whole = lax.all_gather(share, "dp", axis=0, tiled=True).astype(f32)

    def cross(self, value, bits):
        dp, tp = self.dp, self.tp
        route = [(i * tp + t, (i ^ bits[t % 2]) * tp + t) for i in range(dp) for t in range(tp)]
        return lax.ppermute(value, ("dp", "tensor"), route)

    def quarter(self):
        if self.dp != 8:
            return
        rows, d = self.keep.shape
        halves = (2, rows // 2, d)
        send, self.keep = self.call(
            fold_kernel,
            (self.keep.reshape(halves), self.got.reshape(halves)),
            [vspec()] * 2,
            [arr(halves[1:], bf16)] * 2,
            name=self.name + "_half",
        )
        self.got = self.cross(send, (2, 1))

    def middle(self):
        if self.dp != 8:
            return
        self.keep = run_add(self.call, self.keep, self.got, self.name + "_quarter")
        self.got = self.cross(self.keep, (4, 4))

    def back_half(self):
        if self.dp != 8:
            return
        self.keep = run_add(self.call, self.keep, self.got, self.name + "_sum")
        self.got = self.cross(self.keep, (2, 1))

    def back_whole(self):
        if self.dp != 8:
            return
        self.keep = run_join(self.call, 1, self.keep, self.got, bf16, self.name + "_join")
        self.got = self.cross(self.keep, (1, 2))

    def finish(self):
        if self.dp == 8:
            self.whole = run_join(self.call, 0, self.keep, self.got, f32, self.name + "_whole")
        return self.whole


def collect(heads, chunks, *refs):
    width = heads * HEAD
    two, one, exp, attn = (refs[i * chunks : (i + 1) * chunks] for i in range(4))
    norms, rest = refs[4 * chunks :]
    norms[...] = jnp.zeros_like(norms)
    rest[...] = jnp.zeros_like(rest)
    norms[0:3, :] = sum(r[0:3, :] for r in two)
    norms[3:5, :] = sum(r[0:2, :] for r in one)
    rest[0:4, :] = sum(r[0:4, :] for r in exp)
    rest[4:5, 0 : 3 * width] = sum(r[0:1, :] for r in attn)


def stack_kernel(norms, got, rest, out):
    out[0:8, :] = norms[...] + got[...]
    out[8:16, :] = rest[...]


def local(
    dp, tp,
    tokens, token_mask, expert_type, cotangent, ln1_gain, ln1_bias, w_qkv, qv_bias, w_out, out_bias,
    ln2_gain, ln2_bias, w_up, up_bias, w_down, down_bias,
):
    rows, d = tokens.shape
    items = rows // SEQ
    width = w_qkv.shape[2]
    heads = width // HEAD
    core_swap = lambda v: swap(v, "tensor", tp, 1)
    far_swap = lambda v: swap(v, "tensor", tp, 2)
    chunks = items // 2
    call = Order()
    w_t = w_qkv.transpose(1, 2, 0).reshape(3 * width, d)

    def pair_sum(own, other, name):
        pair = run_add(call, own, core_swap(other), name)
        return pair, far_swap(pair)

    o2 = far_swap(w_out)
    outs = (w_out, core_swap(w_out), o2, core_swap(o2))
    totals = run_count_rows(call, items, token_mask, expert_type)
    bit = 1
    ctx, proj, normed_one, ctxs = [], [], [], []
    for k in range(chunks):
        got = swap(totals, "dp", dp, bit) if bit < dp else None
        c0, p, n = run_attention_forward(call, k, heads, token_mask, tokens, w_t, qv_bias, ln1_gain, ln1_bias)
        ctx.append(c0)
        proj.append(p)
        normed_one.append(n)
        c2 = far_swap(c0)
        ctxs.append((c0, core_swap(c0), c2, core_swap(c2)))
        if bit < dp:
            totals = run_add(call, totals, got, "count_%d" % bit)
            bit = 2 * bit
    got = swap(totals, "dp", dp, bit) if bit < dp else None

    middle, masked, normed_two, active, ghid, small_e = [], [], [], [], [], []
    down, part, pairs = [], [], []
    for k in range(chunks):
        m, c, n, a, g, do, dt, po, pt, s = run_experts(
            call, k, heads, token_mask, expert_type, tokens, cotangent, ctxs[k], outs, out_bias, ln2_gain, ln2_bias,
            up_bias, w_up, w_down,
        )
        for group, value in zip(
            (middle, masked, normed_two, active, ghid, down, part, small_e), (m, c, n, a, g, (do, dt), (po, pt), s)
        ):
            group.append(value)
        if k < chunks - 1:
            pairs.append(pair_sum(po, pt, "part_%d" % k))
        if k == 0:
            while bit < dp:
                totals = run_add(call, totals, got, "count_%d" % bit)
                bit = 2 * bit
                got = swap(totals, "dp", dp, bit) if bit < dp else None

    send, keep = run_expert_grads(call, items, expert_type, totals, active, masked, "down_grads")
    sum_down = Sum(call, dp, tp, "down", send, keep)

    grad_mid, branch_own, branch_other, small_n = [None] * chunks, [None] * chunks, [None] * chunks, [None] * chunks
    gproj, small_a, ones = [None] * chunks, [None] * chunks, [None] * chunks

    def norm_two(k):
        grad_mid[k], branch_own[k], small_n[k] = run_norm_two_back(
            call, k, expert_type, totals, middle[k], masked[k], *pairs[k], ln2_gain
        )
        branch_other[k] = core_swap(branch_own[k])

    def attention(k):
        gproj[k], po, pt, small_a[k] = run_attention_backward(
            call, k, heads, token_mask, branch_own[k], branch_other[k], w_out, proj[k], w_t
        )
        ones[k] = (po, pt)

    for k in range(chunks - 1):
        norm_two(k)
    pairs.append(pair_sum(*part[-1], "part_%d" % (chunks - 1)))
    for k in range(chunks - 1):
        attention(k)
    norm_two(chunks - 1)
    sum_down.quarter()
    send, keep = run_expert_grads(call, items, expert_type, totals, normed_two, ghid, "up_grads")
    sum_up = Sum(call, dp, tp, "up", send, keep)
    attention(chunks - 1)
    sum_down.middle()
    send, keep = run_attention_grads(call, items, heads, gproj, normed_one, ctx, branch_own, branch_other)
    pairs_one = [pair_sum(*ones[k], "one_%d" % k) for k in range(chunks)]
    sum_up.quarter()
    sum_attn = Sum(call, dp, tp, "attn", send, keep)
    pairs_down = [pair_sum(*down[k], "out_%d" % k) for k in range(chunks)]
    sum_up.middle()
    sum_attn.quarter()

    grad_own, small_o = [], []
    for k in range(chunks):
        g, s = run_norm_one_back(call, k, tokens, grad_mid[k], *pairs_one[k], ln1_gain)
        grad_own.append(g)
        small_o.append(s)
    grad_other = [core_swap(g) for g in grad_own]
    norms, rest = call(
        functools.partial(collect, heads, chunks),
        (*small_n, *small_o, *small_e, *small_a),
        [vspec()] * (4 * chunks),
        [arr((8, d), f32)] * 2,
        name="collect",
    )
    got_norms = core_swap(norms)
    sum_down.back_half()
    small = call(stack_kernel, (norms, got_norms, rest), [vspec()] * 3, [arr((16, d), f32)], name="stack")[0]
    bit = 1
    got = swap(small, "dp", dp, bit) if bit < dp else None
    sum_attn.middle()
    grad_tokens = run_assemble(call, items, grad_own, grad_other, "grad_tokens")
    sum_down.back_whole()
    out_own = [run_output_rows(call, k, expert_type, middle[k], *pairs_down[k], down_bias) for k in range(chunks)]
    out_other = [core_swap(o) for o in out_own]
    while bit < dp:
        small = run_add(call, small, got, "small_%d" % bit)
        bit = 2 * bit
        got = swap(small, "dp", dp, bit) if bit < dp else None
    output = run_assemble(call, items, out_own, out_other, "output")
    sum_up.back_half()
    grad_down = sum_down.finish()
    sum_up.back_whole()
    sum_attn.back_half()
    sum_attn.back_whole()
    grad_up = sum_up.finish()
    grad_attn = sum_attn.finish()

    both = totals[:2, 0]
    weights = ((both[0] + both[1]) / (2.0 * both))[:, None]
    grad_qkv = grad_attn[: 3 * width].reshape(3, width, d).transpose(2, 0, 1)
    grad_out = grad_attn[3 * width :]
    grad_qv_bias = jnp.stack([small[12, :width], small[12, 2 * width : 3 * width]])
    return (
        output,
        grad_tokens,
        small[3],
        small[4],
        grad_qkv,
        grad_qv_bias,
        grad_out,
        small[2],
        small[0],
        small[1],
        grad_up.reshape(w_up.shape),
        small[8:10] * weights,
        grad_down.reshape(w_down.shape),
        small[10:12] * weights,
        both.astype(jnp.int32),
    )


def solution(mesh):
    in_specs = (
        P("dp", None),
        P("dp"),
        P("dp"),
        P("dp", None),
        P(),
        P(),
        P(None, None, "tensor"),
        P(None, "tensor"),
        P("tensor", None),
        P(),
        P(),
        P(),
        P(None, None, "tensor"),
        P(None, "tensor"),
        P(None, "tensor", None),
        P(),
    )
    out_specs = (
        P("dp", None),
        P("dp", None),
        P(),
        P(),
        P(None, None, "tensor"),
        P(None, "tensor"),
        P("tensor", None),
        P(),
        P(),
        P(),
        P(None, None, "tensor"),
        P(None, "tensor"),
        P(None, "tensor", None),
        P(),
        P(),
    )
    return jax.shard_map(
        functools.partial(local, mesh.shape["dp"], mesh.shape["tensor"]),
        mesh=mesh,
        in_specs=in_specs,
        out_specs=out_specs,
        check_vma=False,
    )
```

time: 484 us -> 249 us (0.51); the launches traced: 475 us -> 245 us
  waiting for transfers between devices: 328 us -> 119 us
  other arithmetic: 18.2 us -> 2 us
  between operations: 17.7 us -> 2.67 us
  starting transfers between devices: 24.9 us -> 38.4 us
  local copies, waits for them, and re-layouts: 30.9 us -> 20.5 us
  Pallas kernels: 55.1 us -> 62.9 us
    reduce_scatter x3 -> x0, waiting for transfers between devices: 192 us -> none  [sum_over_items(): share = lax.psum_scatter(flat, 'dp', scatter_dimension=0, tiled=True)]
    all_gather x3 -> x0, waiting for transfers between devices: 88.2 us -> none  [sum_over_items(): lax.all_gather(share, 'dp', axis=0, tiled=True).reshape(piece.shape)]
    ppermute x0 -> x15, waiting for transfers between devices: none -> 65.4 us  [cross(): return lax.ppermute(value, ('dp', 'tensor'), route)]
    ppermute x0 -> x15, starting transfers between devices: none -> 19 us  [cross(): return lax.ppermute(value, ('dp', 'tensor'), route)]
    convert_element_type x10 -> x1, other arithmetic: 13.3 us -> 0.63 us  [local(): both.astype(jnp.int32)]
    pallas_call x17 -> x47, Pallas kernels: 55.1 us -> 62.9 us  [__call__(): pl.pallas_call(body, out_shape=list(outs), in_specs=list(specs) + [aspec(...]
    ppermute x34, waiting for transfers between devices: 47.5 us -> 53.4 us  [swap(): return lax.ppermute(value, axis, [(i, i ^ bit) for i in range(size)])]
    ppermute x34, starting transfers between devices: 24.4 us -> 19.4 us  [swap(): return lax.ppermute(value, axis, [(i, i ^ bit) for i in range(size)])]
  transfers between devices with their start and end apart: 40 -> 49, of which waited for: 16 -> 22; matrix products, arithmetic and copies ran while one was open for 5% -> 1% of each run, Pallas kernels for 10% -> 15%
where the time goes in v2:
time: 249 us; the launch traced here: 245 us
  waiting for transfers between devices  119 us (48%)
  Pallas kernels  62.9 us (25%)
  starting transfers between devices  38.4 us (15%)
  local copies, waits for them, and re-layouts  20.5 us (8%)
  between operations  2.67 us (1%)
    ppermute x15, waiting for transfers between devices, cross(): return lax.ppermute(value, ('dp', 'tensor'), route)  65.4 us
    pallas_call x47, Pallas kernels, __call__(): pl.pallas_call(body, out_shape=list(outs), in_specs=list(specs) + [aspec(...  62.9 us
    ppermute x34, waiting for transfers between devices, swap(): return lax.ppermute(value, axis, [(i, i ^ bit) for i in range(size)])  53.4 us
    ppermute x34, starting transfers between devices, swap(): return lax.ppermute(value, axis, [(i, i ^ bit) for i in range(size)])  19.4 us
    ppermute x15, starting transfers between devices, cross(): return lax.ppermute(value, ('dp', 'tensor'), route)  19 us
    unnamed x54, local copies, waits for them, and re-layouts  17.2 us
  transfers between devices with their start and end apart: 49, of which 22 were waited for; matrix products, arithmetic and copies ran while one was open for 1% of the time, Pallas kernels for 15%

profile of v2, /device:TPU:0, one launch (start us, length us, event | category | flops | bytes accessed | tf_op | source)
XLA Modules:
  0.0 245.2 jit_solution(18132709442670327368)
XLA Ops:
  0.6 3.0 %collective-permute-start.4 = (bf16[192,768]{1,0:T(8,128)(2,1)}, bf16[192,768]{1,0:T(8,128)(2,1)S(1)}, u32[]{:S(2)}, u32[]{:S(2)}) collective-permute-start(bf16[192,768]{1,0:T(8,128)(2,1)} %refs_3_.11), channel_id=1, source_target_pairs={{0,2},{1,3},{2,0},{3,1},{4,6},{5,7},{6,4},{7,5},{8,10},{9,11},{10,... | collective-permute-start | bytes 884744 | tf_op jit(solution)/shard_map/ppermute | solution.py:514
  11.1 3.5 %attention_forward_0.1 = (bf16[240,384]{1,0:T(8,128)(2,1)S(1)}, bf16[2,240,576]{2,1,0:T(8,128)(2,1)S(1)}, bf16[2,240,768]{2,1,0:T(8,128)(2,1)S(1)}) custom-call(s32[948]{0:T(1024)S(1)} %copy-done.16, bf16[948,768]{1,0:T(8,128)(2,1)S(1)} %copy-done.2, bf16[576,768]{1,0:T(8,128)(2,1)S(1)} %bitcast.29, f32[2,192]{1,0:T(2,128)S(1)} %copy-done.25, ...), custom_call_target="tpu_custom_call" | custom-call | flops 654311424 | bytes 3826896 | tf_op jit(solution)/shard_map/attention_forward_0/pallas_call | solution.py:81
  15.5 5.4 %collective-permute-done.1.refs_6_ = bf16[240,384]{1,0:T(8,128)(2,1)S(1)} collective-permute-done((bf16[240,384]{1,0:T(8,128)(2,1)S(1)}, bf16[240,384]{1,0:T(8,128)(2,1)S(1)}, u32[]{:S(2)}, u32[]{:S(2)}) %collective-permute-start.1) | collective-permute-done | bytes 184352 | tf_op jit(solution)/shard_map/ppermute | solution.py:514
  26.1 3.5 %attention_forward_1.1 = (bf16[240,384]{1,0:T(8,128)(2,1)S(1)}, bf16[2,240,576]{2,1,0:T(8,128)(2,1)S(1)}, bf16[2,240,768]{2,1,0:T(8,128)(2,1)S(1)}) custom-call(s32[948]{0:T(1024)S(1)} %copy-done.16, bf16[948,768]{1,0:T(8,128)(2,1)S(1)} %copy-done.3, bf16[576,768]{1,0:T(8,128)(2,1)S(1)} %bitcast.30, f32[2,192]{1,0:T(2,128)S(1)} %copy-done.26, ...), custom_call_target="tpu_custom_call" | custom-call | flops 654311424 | bytes 3826896 | tf_op jit(solution)/shard_map/attention_forward_1/pallas_call | solution.py:81
  32.8 5.2 %experts_0.1 = (f32[240,768]{1,0:T(8,128)S(1)}, bf16[2,240,768]{2,1,0:T(8,128)(2,1)S(1)}, bf16[2,240,768]{2,1,0:T(8,128)(2,1)S(1)}, bf16[2,240,768]{2,1,0:T(8,12...) custom-call(s32[948]{0:T(1024)S(1)} %copy-done.17, ...), custom_call_target="tpu_custom_call" | custom-call | flops 2831155200 | bytes 14756256 | tf_op jit(solution)/shard_map/experts_0/pallas_call | solution.py:81
  38.9 6.3 %collective-permute-done.12.refs_6_ = bf16[240,384]{1,0:T(8,128)(2,1)S(1)} collective-permute-done((bf16[240,384]{1,0:T(8,128)(2,1)S(1)}, bf16[240,384]{1,0:T(8,128)(2,1)S(1)}, u32[]{:S(2)}, u32[]{:S(2)}) %collective-permute-start.12) | collective-permute-done | bytes 184352 | tf_op jit(solution)/shard_map/ppermute | solution.py:514
  49.7 5.5 %experts_1.1 = (f32[240,768]{1,0:T(8,128)S(1)}, bf16[2,240,768]{2,1,0:T(8,128)(2,1)S(1)}, bf16[2,240,768]{2,1,0:T(8,128)(2,1)S(1)}, bf16[2,240,768]{2,1,0:T(8,12...) custom-call(s32[948]{0:T(1024)S(1)} %copy-done.17, ...), custom_call_target="tpu_custom_call" | custom-call | flops 2831155200 | bytes 14756256 | tf_op jit(solution)/shard_map/experts_1/pallas_call | solution.py:81
  55.3 2.9 %down_grads.1 = (bf16[768,768]{1,0:T(8,128)(2,1)S(1)}, bf16[768,768]{1,0:T(8,128)(2,1)S(1)}) custom-call(s32[948]{0:T(1024)S(1)} %copy-done.10, f32[8,128]{1,0:T(8,128)S(1)} %count_4.1.refs_18_.refs_1_, bf16[2,240,768]{2,1,0:T(8,128)(2,1)S(1)} %get-tuple-element.84.refs_2_, bf16[2,240,768]{2,1,0:T(8,128)(2,1)S(1)} %get-tuple-element.85.refs_3_, ...), custom_call_target="tpu_custom_call" | custom-call | flops 1132462080 | bytes 5316304 | tf_op jit(solution)/shard_map/down_grads/pallas_call | solution.py:81
  60.2 8.0 %collective-permute-done.16.refs_5_ = bf16[240,768]{1,0:T(8,128)(2,1)S(1)} collective-permute-done((bf16[240,768]{1,0:T(8,128)(2,1)S(1)}, bf16[240,768]{1,0:T(8,128)(2,1)S(1)}, u32[]{:S(2)}, u32[]{:S(2)}) %collective-permute-start.16) | collective-permute-done | bytes 368672 | tf_op jit(solution)/shard_map/ppermute | solution.py:514
  71.3 5.2 %attention_backward_0.1 = (bf16[2,240,576]{2,1,0:T(8,128)(2,1)S(1)}, bf16[240,768]{1,0:T(8,128)(2,1)S(1)}, bf16[240,768]{1,0:T(8,128)(2,1)S(1)}, f32[8,576]{1,0:T(8,128)S(1)}) custom-call(s32[948]{0:T(1024)S(1)} %copy-done.17, bf16[240,768]{1,0:T(8,128)(2,1)S(1)} %get-tuple-element.94.refs_1_.refs_6_, ...), custom_call_target="tpu_custom_call" | custom-call | flops 787415040 | bytes 3782352 | tf_op jit(solution)/shard_map/attention_backward_0/pallas_call | solution.py:81
  76.5 4.3 %collective-permute-done.17.refs_5_ = bf16[240,768]{1,0:T(8,128)(2,1)S(1)} collective-permute-done((bf16[240,768]{1,0:T(8,128)(2,1)S(1)}, bf16[240,768]{1,0:T(8,128)(2,1)S(1)}, u32[]{:S(2)}, u32[]{:S(2)}) %collective-permute-start.17) | collective-permute-done | bytes 368672 | tf_op jit(solution)/shard_map/ppermute | solution.py:514
  82.4 13.0 %up_grads.1 = (bf16[768,768]{1,0:T(8,128)(2,1)S(1)}, bf16[768,768]{1,0:T(8,128)(2,1)S(1)}) custom-call(s32[948]{0:T(1024)S(1)} %copy-done.10, f32[8,128]{1,0:T(8,128)S(1)} %count_4.1.refs_18_.refs_1_, bf16[2,240,768]{2,1,0:T(8,128)(2,1)S(1)} %get-tuple-element.80.refs_2_, bf16[2,240,768]{2,1,0:T(8,128)(2,1)S(1)} %get-tuple-element.81.refs_3_, ...), custom_call_target="tpu_custom_call" | custom-call | flops 1132462080 | bytes 5316304 | tf_op jit(solution)/shard_map/up_grads/pallas_call | solution.py:81
  98.7 5.2 %attention_backward_1.1 = (bf16[2,240,576]{2,1,0:T(8,128)(2,1)S(1)}, bf16[240,768]{1,0:T(8,128)(2,1)S(1)}, bf16[240,768]{1,0:T(8,128)(2,1)S(1)}, f32[8,576]{1,0:T(8,128)S(1)}) custom-call(s32[948]{0:T(1024)S(1)} %copy-done.17, bf16[240,768]{1,0:T(8,128)(2,1)S(1)} %get-tuple-element.101.refs_1_.refs_7_, ...), custom_call_target="tpu_custom_call" | custom-call | flops 787415040 | bytes 3782352 | tf_op jit(solution)/shard_map/attention_backward_1/pallas_call | solution.py:81
  104.5 8.8 %collective-permute-done.23.refs_1_ = bf16[384,768]{1,0:T(8,128)(2,1)S(1)} collective-permute-done((bf16[384,768]{1,0:T(8,128)(2,1)S(1)}, bf16[384,768]{1,0:T(8,128)(2,1)S(1)}, u32[]{:S(2)}, u32[]{:S(2)}) %collective-permute-start.23) | collective-permute-done | bytes 589856 | tf_op jit(solution)/shard_map/ppermute | solution.py:558
  126.2 19.9 %collective-permute-done.28.refs_1_ = bf16[384,768]{1,0:T(8,128)(2,1)S(1)} collective-permute-done((bf16[384,768]{1,0:T(8,128)(2,1)S(1)}, bf16[384,768]{1,0:T(8,128)(2,1)S(1)}, u32[]{:S(2)}, u32[]{:S(2)}) %collective-permute-start.28) | collective-permute-done | bytes 589856 | tf_op jit(solution)/shard_map/ppermute | solution.py:558
  153.5 8.2 %collective-permute-done.34.refs_1_ = bf16[192,768]{1,0:T(8,128)(2,1)S(1)} collective-permute-done((bf16[192,768]{1,0:T(8,128)(2,1)S(1)}, bf16[192,768]{1,0:T(8,128)(2,1)S(1)}, u32[]{:S(2)}, u32[]{:S(2)}) %collective-permute-start.34) | collective-permute-done | bytes 294944 | tf_op jit(solution)/shard_map/ppermute | solution.py:558
  168.0 3.6 %collective-permute-done.36.refs_3_ = bf16[240,768]{1,0:T(8,128)(2,1)S(1)} collective-permute-done((bf16[240,768]{1,0:T(8,128)(2,1)S(1)}, bf16[240,768]{1,0:T(8,128)(2,1)S(1)}, u32[]{:S(2)}, u32[]{:S(2)}) %collective-permute-start.36) | collective-permute-done | bytes 368672 | tf_op jit(solution)/shard_map/ppermute | solution.py:514
  173.4 10.5 %collective-permute-done.39.refs_1_ = f32[16,768]{1,0:T(8,128)S(1)} collective-permute-done((f32[16,768]{1,0:T(8,128)S(1)}, f32[16,768]{1,0:T(8,128)S(1)}, u32[]{:S(2)}, u32[]{:S(2)}) %collective-permute-start.39) | collective-permute-done | bytes 49184 | tf_op jit(solution)/shard_map/ppermute | solution.py:514
  186.0 3.9 %collective-permute-done.40.refs_1_ = f32[16,768]{1,0:T(8,128)S(1)} collective-permute-done((f32[16,768]{1,0:T(8,128)S(1)}, f32[16,768]{1,0:T(8,128)S(1)}, u32[]{:S(2)}, u32[]{:S(2)}) %collective-permute-start.40) | collective-permute-done | bytes 49184 | tf_op jit(solution)/shard_map/ppermute | solution.py:514
  190.6 4.5 %collective-permute-done.41.refs_1_ = f32[16,768]{1,0:T(8,128)S(1)} collective-permute-done((f32[16,768]{1,0:T(8,128)S(1)}, f32[16,768]{1,0:T(8,128)S(1)}, u32[]{:S(2)}, u32[]{:S(2)}) %collective-permute-start.41) | collective-permute-done | bytes 49184 | tf_op jit(solution)/shard_map/ppermute | solution.py:514
  203.4 10.3 %collective-permute-done.44.refs_1_ = bf16[384,768]{1,0:T(8,128)(2,1)S(1)} collective-permute-done((bf16[384,768]{1,0:T(8,128)(2,1)S(1)}, bf16[384,768]{1,0:T(8,128)(2,1)S(1)}, u32[]{:S(2)}, u32[]{:S(2)}) %collective-permute-start.44) | collective-permute-done | bytes 589856 | tf_op jit(solution)/shard_map/ppermute | solution.py:558
  219.4 7.4 %collective-permute-done.46.refs_1_ = bf16[192,768]{1,0:T(8,128)(2,1)S(1)} collective-permute-done((bf16[192,768]{1,0:T(8,128)(2,1)S(1)}, bf16[192,768]{1,0:T(8,128)(2,1)S(1)}, u32[]{:S(2)}, u32[]{:S(2)}) %collective-permute-start.46) | collective-permute-done | bytes 294944 | tf_op jit(solution)/shard_map/ppermute | solution.py:558
  230.3 3.7 %collective-permute-done.48.refs_1_ = bf16[768,768]{1,0:T(8,128)(2,1)S(1)} collective-permute-done((bf16[768,768]{1,0:T(8,128)(2,1)S(1)}, bf16[768,768]{1,0:T(8,128)(2,1)S(1)}, u32[]{:S(2)}, u32[]{:S(2)}) %collective-permute-start.48) | collective-permute-done | bytes 1179680 | tf_op jit(solution)/shard_map/ppermute | solution.py:558
  236.5 3.8 %collective-permute-done.47.refs_1_ = bf16[384,768]{1,0:T(8,128)(2,1)S(1)} collective-permute-done((bf16[384,768]{1,0:T(8,128)(2,1)S(1)}, bf16[384,768]{1,0:T(8,128)(2,1)S(1)}, u32[]{:S(2)}, u32[]{:S(2)}) %collective-permute-start.47) | collective-permute-done | bytes 589856 | tf_op jit(solution)/shard_map/ppermute | solution.py:558
  (184 shorter events, 86.7 us)
Async XLA Ops:
  0.6 14.3 %collective-permute-start.4 = (bf16[192,768]{1,0:T(8,128)(2,1)}, bf16[192,768]{1,0:T(8,128)(2,1)S(1)}, u32[]{:S(2)}, u32[]{:S(2)}) collective-permute-start(bf16[192,768]{1,0:T(8,128)(2,1)} %refs_3_.11), channel_id=1, source_target_pairs={{0,2},{1,3},{2,0},{3,1},{4,6},{5,7},{6,4},{7,5},{8,10},{9,11},{10,... | collective-permute-start | bytes 884744 | tf_op jit(solution)/shard_map/ppermute | solution.py:514
  14.8 14.8 %collective-permute-start.3 = (bf16[192,768]{1,0:T(8,128)(2,1)}, bf16[192,768]{1,0:T(8,128)(2,1)S(1)}, u32[]{:S(2)}, u32[]{:S(2)}) collective-permute-start(bf16[192,768]{1,0:T(8,128)(2,1)} %refs_3_.11), channel_id=1, source_target_pairs={{0,1},{1,0},{2,3},{3,2},{4,5},{5,4},{6,7},{7,6},{8,9},{9,8},{10,11... | collective-permute-start | bytes 884744 | tf_op jit(solution)/shard_map/ppermute | solution.py:514
  14.9 14.8 %collective-permute-start.5 = (bf16[192,768]{1,0:T(8,128)(2,1)S(1)}, bf16[192,768]{1,0:T(8,128)(2,1)S(1)}, u32[]{:S(2)}, u32[]{:S(2)}) collective-permute-start(bf16[192,768]{1,0:T(8,128)(2,1)S(1)} %collective-permute-done.4.refs_10_), channel_id=1, source_target_pairs={{0,1},{1,0},{2,3},{3,2},{4,5},{5,4},{6,7},{7,6},{8,9},{9,8},{10,11... | collective-permute-start | bytes 884744 | tf_op jit(solution)/shard_map/ppermute | solution.py:514
  15.4 14.3 %collective-permute-start = (bf16[240,384]{1,0:T(8,128)(2,1)S(1)}, bf16[240,384]{1,0:T(8,128)(2,1)S(1)}, u32[]{:S(2)}, u32[]{:S(2)}) collective-permute-start(bf16[240,384]{1,0:T(8,128)(2,1)S(1)} %get-tuple-element.73.refs_2_.refs_4_), channel_id=1, source_target_pairs={{0,1},{1,0},{2,3},{3,2},{4,5},{5,4},{6,7},{7,6},{8,9},{9,8},{10,11... | collective-permute-start | bytes 552968 | tf_op jit(solution)/shard_map/ppermute | solution.py:514
  58.2 24.0 %collective-permute-start.14 = (bf16[768,768]{1,0:T(8,128)(2,1)S(1)}, bf16[768,768]{1,0:T(8,128)(2,1)S(1)}, u32[]{:S(2)}, u32[]{:S(2)}) collective-permute-start(bf16[768,768]{1,0:T(8,128)(2,1)S(1)} %get-tuple-element.90.refs_7_), channel_id=1, source_target_pairs={{0,4},{1,9},{2,6},{3,11},{4,0},{5,13},{6,2},{7,15},{8,12},{9,1},{1... | collective-permute-start | bytes 3538952 | tf_op jit(solution)/shard_map/ppermute | solution.py:558
  95.4 22.6 %collective-permute-start.19 = (bf16[768,768]{1,0:T(8,128)(2,1)S(1)}, bf16[768,768]{1,0:T(8,128)(2,1)S(1)}, u32[]{:S(2)}, u32[]{:S(2)}) collective-permute-start(bf16[768,768]{1,0:T(8,128)(2,1)S(1)} %get-tuple-element.100.refs_6_), channel_id=1, source_target_pairs={{0,4},{1,9},{2,6},{3,11},{4,0},{5,13},{6,2},{7,15},{8,12},{9,1},{1... | collective-permute-start | bytes 3538952 | tf_op jit(solution)/shard_map/ppermute | solution.py:558
  97.0 16.3 %collective-permute-start.23 = (bf16[384,768]{1,0:T(8,128)(2,1)S(1)}, bf16[384,768]{1,0:T(8,128)(2,1)S(1)}, u32[]{:S(2)}, u32[]{:S(2)}) collective-permute-start(bf16[384,768]{1,0:T(8,128)(2,1)S(1)} %get-tuple-element.98.refs_6_), channel_id=1, source_target_pairs={{0,8},{1,5},{2,10},{3,7},{4,12},{5,1},{6,14},{7,3},{8,0},{9,13},{1... | collective-permute-start | bytes 1769480 | tf_op jit(solution)/shard_map/ppermute | solution.py:558
  98.6 16.5 %collective-permute-start.22 = (bf16[240,768]{1,0:T(8,128)(2,1)S(1)}, bf16[240,768]{1,0:T(8,128)(2,1)S(1)}, u32[]{:S(2)}, u32[]{:S(2)}) collective-permute-start(bf16[240,768]{1,0:T(8,128)(2,1)S(1)} %get-tuple-element.106), channel_id=1, source_target_pairs={{0,1},{1,0},{2,3},{3,2},{4,5},{5,4},{6,7},{7,6},{8,9},{9,8},{10,11... | collective-permute-start | bytes 1105928 | tf_op jit(solution)/shard_map/ppermute | solution.py:514
  104.4 19.7 %collective-permute-start.8 = (bf16[240,768]{1,0:T(8,128)(2,1)S(1)}, bf16[240,768]{1,0:T(8,128)(2,1)S(1)}, u32[]{:S(2)}, u32[]{:S(2)}) collective-permute-start(bf16[240,768]{1,0:T(8,128)(2,1)S(1)} %get-tuple-element.77), channel_id=1, source_target_pairs={{0,1},{1,0},{2,3},{3,2},{4,5},{5,4},{6,7},{7,6},{8,9},{9,8},{10,11... | collective-permute-start | bytes 1105928 | tf_op jit(solution)/shard_map/ppermute | solution.py:514
  118.3 27.9 %collective-permute-start.28 = (bf16[384,768]{1,0:T(8,128)(2,1)S(1)}, bf16[384,768]{1,0:T(8,128)(2,1)S(1)}, u32[]{:S(2)}, u32[]{:S(2)}) collective-permute-start(bf16[384,768]{1,0:T(8,128)(2,1)S(1)} %get-tuple-element.112.refs_2_), channel_id=1, source_target_pairs={{0,8},{1,5},{2,10},{3,7},{4,12},{5,1},{6,14},{7,3},{8,0},{9,13},{1... | collective-permute-start | bytes 1769480 | tf_op jit(solution)/shard_map/ppermute | solution.py:558
  119.9 26.4 %collective-permute-start.27 = (bf16[384,768]{1,0:T(8,128)(2,1)S(1)}, bf16[384,768]{1,0:T(8,128)(2,1)S(1)}, u32[]{:S(2)}, u32[]{:S(2)}) collective-permute-start(bf16[384,768]{1,0:T(8,128)(2,1)S(1)} %get-tuple-element.111.refs_2_), channel_id=1, source_target_pairs={{0,4},{1,9},{2,6},{3,11},{4,0},{5,13},{6,2},{7,15},{8,12},{9,1},{1... | collective-permute-start | bytes 1769480 | tf_op jit(solution)/shard_map/ppermute | solution.py:558
  121.4 27.1 %collective-permute-start.25 = (bf16[384,768]{1,0:T(8,128)(2,1)S(1)}, bf16[384,768]{1,0:T(8,128)(2,1)S(1)}, u32[]{:S(2)}, u32[]{:S(2)}) collective-permute-start(bf16[384,768]{1,0:T(8,128)(2,1)S(1)} %down_quarter.1.refs_10_.refs_0_), channel_id=1, source_target_pairs={{0,16},{1,17},{2,18},{3,19},{4,20},{5,21},{6,22},{7,23},{8,24},{9,... | collective-permute-start | bytes 1769480 | tf_op jit(solution)/shard_map/ppermute | solution.py:558
  124.0 22.5 %collective-permute-start.26 = (bf16[240,768]{1,0:T(8,128)(2,1)S(1)}, bf16[240,768]{1,0:T(8,128)(2,1)S(1)}, u32[]{:S(2)}, u32[]{:S(2)}) collective-permute-start(bf16[240,768]{1,0:T(8,128)(2,1)S(1)} %one_0.1.refs_2_), channel_id=1, source_target_pairs={{0,2},{1,3},{2,0},{3,1},{4,6},{5,7},{6,4},{7,5},{8,10},{9,11},{10,... | collective-permute-start | bytes 1105928 | tf_op jit(solution)/shard_map/ppermute | solution.py:514
  124.5 22.7 %collective-permute-start.30 = (bf16[240,768]{1,0:T(8,128)(2,1)S(1)}, bf16[240,768]{1,0:T(8,128)(2,1)S(1)}, u32[]{:S(2)}, u32[]{:S(2)}) collective-permute-start(bf16[240,768]{1,0:T(8,128)(2,1)S(1)} %one_1.1.refs_2_), channel_id=1, source_target_pairs={{0,2},{1,3},{2,0},{3,1},{4,6},{5,7},{6,4},{7,5},{8,10},{9,11},{10,... | collective-permute-start | bytes 1105928 | tf_op jit(solution)/shard_map/ppermute | solution.py:514
  148.7 16.5 %collective-permute-start.31 = (bf16[384,768]{1,0:T(8,128)(2,1)S(1)}, bf16[384,768]{1,0:T(8,128)(2,1)S(1)}, u32[]{:S(2)}, u32[]{:S(2)}) collective-permute-start(bf16[384,768]{1,0:T(8,128)(2,1)S(1)} %down_sum.1.refs_3_.refs_0_), channel_id=1, source_target_pairs={{0,8},{1,5},{2,10},{3,7},{4,12},{5,1},{6,14},{7,3},{8,0},{9,13},{1... | collective-permute-start | bytes 1769480 | tf_op jit(solution)/shard_map/ppermute | solution.py:558
  153.0 14.2 %collective-permute-start.24 = (bf16[240,768]{1,0:T(8,128)(2,1)S(1)}, bf16[240,768]{1,0:T(8,128)(2,1)S(1)}, u32[]{:S(2)}, u32[]{:S(2)}) collective-permute-start(bf16[240,768]{1,0:T(8,128)(2,1)S(1)} %out_0.1.refs_2_), channel_id=1, source_target_pairs={{0,2},{1,3},{2,0},{3,1},{4,6},{5,7},{6,4},{7,5},{8,10},{9,11},{10,... | collective-permute-start | bytes 1105928 | tf_op jit(solution)/shard_map/ppermute | solution.py:514
  162.4 34.4 %collective-permute-start.43 = (bf16[384,768]{1,0:T(8,128)(2,1)S(1)}, bf16[384,768]{1,0:T(8,128)(2,1)S(1)}, u32[]{:S(2)}, u32[]{:S(2)}) collective-permute-start(bf16[384,768]{1,0:T(8,128)(2,1)S(1)} %up_quarter.1.refs_2_.refs_0_), channel_id=1, source_target_pairs={{0,16},{1,17},{2,18},{3,19},{4,20},{5,21},{6,22},{7,23},{8,24},{9,... | collective-permute-start | bytes 1769480 | tf_op jit(solution)/shard_map/ppermute | solution.py:558
  166.6 34.3 %collective-permute-start.45 = (bf16[768,768]{1,0:T(8,128)(2,1)S(1)}, bf16[768,768]{1,0:T(8,128)(2,1)S(1)}, u32[]{:S(2)}, u32[]{:S(2)}) collective-permute-start(bf16[768,768]{1,0:T(8,128)(2,1)S(1)} %bitcast.19), channel_id=1, source_target_pairs={{0,4},{1,9},{2,6},{3,11},{4,0},{5,13},{6,2},{7,15},{8,12},{9,1},{1... | collective-permute-start | bytes 3538952 | tf_op jit(solution)/shard_map/ppermute | solution.py:558
  172.3 22.8 %collective-permute-start.38 = (bf16[240,768]{1,0:T(8,128)(2,1)S(1)}, bf16[240,768]{1,0:T(8,128)(2,1)S(1)}, u32[]{:S(2)}, u32[]{:S(2)}) collective-permute-start(bf16[240,768]{1,0:T(8,128)(2,1)S(1)} %output_rows_1.1.refs_2_.refs_1_), channel_id=1, source_target_pairs={{0,1},{1,0},{2,3},{3,2},{4,5},{5,4},{6,7},{7,6},{8,9},{9,8},{10,11... | collective-permute-start | bytes 1105928 | tf_op jit(solution)/shard_map/ppermute | solution.py:514
  172.4 22.8 %collective-permute-start.37 = (bf16[240,768]{1,0:T(8,128)(2,1)S(1)}, bf16[240,768]{1,0:T(8,128)(2,1)S(1)}, u32[]{:S(2)}, u32[]{:S(2)}) collective-permute-start(bf16[240,768]{1,0:T(8,128)(2,1)S(1)} %output_rows_0.1.refs_5_.refs_0_), channel_id=1, source_target_pairs={{0,1},{1,0},{2,3},{3,2},{4,5},{5,4},{6,7},{7,6},{8,9},{9,8},{10,11... | collective-permute-start | bytes 1105928 | tf_op jit(solution)/shard_map/ppermute | solution.py:514
  198.3 15.4 %collective-permute-start.44 = (bf16[384,768]{1,0:T(8,128)(2,1)S(1)}, bf16[384,768]{1,0:T(8,128)(2,1)S(1)}, u32[]{:S(2)}, u32[]{:S(2)}) collective-permute-start(bf16[384,768]{1,0:T(8,128)(2,1)S(1)} %up_sum.1.refs_2_.refs_0_), channel_id=1, source_target_pairs={{0,8},{1,5},{2,10},{3,7},{4,12},{5,1},{6,14},{7,3},{8,0},{9,13},{1... | collective-permute-start | bytes 1769480 | tf_op jit(solution)/shard_map/ppermute | solution.py:558
  198.4 18.3 %collective-permute-start.42 = (bf16[192,768]{1,0:T(8,128)(2,1)S(1)}, bf16[192,768]{1,0:T(8,128)(2,1)S(1)}, u32[]{:S(2)}, u32[]{:S(2)}) collective-permute-start(bf16[192,768]{1,0:T(8,128)(2,1)S(1)} %attn_quarter.1.refs_4_.refs_0_), channel_id=1, source_target_pairs={{0,16},{1,17},{2,18},{3,19},{4,20},{5,21},{6,22},{7,23},{8,24},{9,... | collective-permute-start | bytes 884744 | tf_op jit(solution)/shard_map/ppermute | solution.py:558
  216.1 17.9 %collective-permute-start.48 = (bf16[768,768]{1,0:T(8,128)(2,1)S(1)}, bf16[768,768]{1,0:T(8,128)(2,1)S(1)}, u32[]{:S(2)}, u32[]{:S(2)}) collective-permute-start(bf16[768,768]{1,0:T(8,128)(2,1)S(1)} %bitcast.17), channel_id=1, source_target_pairs={{0,4},{1,9},{2,6},{3,11},{4,0},{5,13},{6,2},{7,15},{8,12},{9,1},{1... | collective-permute-start | bytes 3538952 | tf_op jit(solution)/shard_map/ppermute | solution.py:558
  226.8 13.5 %collective-permute-start.47 = (bf16[384,768]{1,0:T(8,128)(2,1)S(1)}, bf16[384,768]{1,0:T(8,128)(2,1)S(1)}, u32[]{:S(2)}, u32[]{:S(2)}) collective-permute-start(bf16[384,768]{1,0:T(8,128)(2,1)S(1)} %bitcast.23), channel_id=1, source_target_pairs={{0,4},{1,9},{2,6},{3,11},{4,0},{5,13},{6,2},{7,15},{8,12},{9,1},{1... | collective-permute-start | bytes 1769480 | tf_op jit(solution)/shard_map/ppermute | solution.py:558
  (52 other events, 406.5 us)
